TPU v7x, 512 devices: a whole 4x8x8 slice. The times are simulated.
512 devices in a mesh: stn: 32 (over x, z), cell: 16 (over y, core).
Axes of the slice: x: 4, y: 8, z: 8, core: 2. Of those that a mesh axis runs over, the one named last changes fastest.
Arguments:
- sensitivity: bfloat16 [32, 16, 2, 512, 512], P('stn', 'cell'), may hold values from -0.046875 to 0.046875
- block_list: int32 [32, 16, 2], P('stn', 'cell'), may hold values from 0 to 63, as said below
- margin: int32 [1024, 4], P('cell'), may hold values from 0 to 31, as said below
- centres: int32 [16, 1024], P('cell'), may hold values from 0 to 32767
- controls: float32 [16384, 128], P(('stn', 'cell')), may hold values from -4 to 4
- observed: float32 [16384, 128], P(('stn', 'cell')), may hold values from -6 to 6
Outputs:
- updated: float32 [16384, 128], P(('stn', 'cell'))
- residual: float32 [16384, 128], P(('stn', 'cell'))
Inputs may be any that keep to these rules, and one draw needn't show every extreme that they name: `block_list`: the 2 cell blocks of one device are distinct. `margin`: the 4 control blocks listed for one cell block are distinct.
All inputs are finite; a program needn't handle non-finite values.
Results may differ from a plain program's by a relative error of at most 0.0003.
Values sent between devices are 32-bit elements; how exact they have to be, the bound alone decides.
A program may use at most 64 MiB of HBM per device.

v0:
```python
import jax
import jax.numpy as jnp
from jax import lax
from jax.sharding import PartitionSpec as P

ITERS = 3


rbf_radius = 10.0


def gaussian(cell_ids, centre_ids):
    squared = jnp.zeros(cell_ids.shape + (centre_ids.shape[-1],), jnp.float32)
    for divisor, modulus in ((1024, 1073741824), (32, 32), (1, 32)):
        cell_coord = (cell_ids // divisor % modulus).astype(jnp.float32)
        centre_coord = (centre_ids // divisor % modulus).astype(jnp.float32)
        spread = cell_coord[..., :, None] - centre_coord[..., None, :]
        squared = squared + spread * spread
    return jnp.exp(squared * (-0.5 / (rbf_radius * rbf_radius)))


def slot_basis(blocks, margin_rows, centre_row, block_size, centre_count):
    offsets = jnp.arange(block_size, dtype=jnp.int32)
    cell_ids = blocks[:, None] * block_size + offsets[None, :]
    listed = margin_rows[blocks]
    within = jnp.arange(centre_count, dtype=jnp.int32)
    slot_ids = listed[:, :, None] * centre_count + within[None, None, :]
    centre_ids = centre_row[slot_ids.reshape(blocks.shape[0], -1)]
    return gaussian(cell_ids, centre_ids)


def local(sensitivity, block_list, margin, centres, controls, observed):
    sens_blocks = sensitivity[0, 0].astype(jnp.float32)
    blocks = block_list[0, 0]
    slot_count = sens_blocks.shape[0]
    block_size = sens_blocks.shape[1]
    centre_count = controls.shape[0]
    members = controls.shape[1]
    stn_count = lax.axis_size("stn")
    basis_table = slot_basis(blocks, margin, centres[0], block_size, centre_count)
    listed = margin[blocks]
    onehot = (listed[:, :, None] == jnp.arange(stn_count, dtype=jnp.int32)[None, None, :]).astype(
        jnp.float32
    )

    def cell_field(group_coeffs):
        picked = group_coeffs.reshape(stn_count, centre_count, members)[listed]
        picked = picked.reshape(slot_count, -1, members)
        return jnp.einsum("nib,nbk->nik", basis_table, picked, precision=lax.Precision.HIGHEST)

    def group_rows(vector):
        return lax.all_gather(vector, "stn", axis=0, tiled=True)

    def station_part(values):
        return jnp.einsum("nij,njk->ik", sens_blocks, values, precision=lax.Precision.HIGHEST)

    def station_sum(partial_rows):
        return lax.psum_scatter(partial_rows, "cell", scatter_dimension=0, tiled=True)

    def full_rows(residual):
        return lax.all_gather(residual, "cell", axis=0, tiled=True)

    def control_total(grouped):
        return lax.psum_scatter(grouped, "stn", scatter_dimension=0, tiled=True)

    def control_square(gradient):
        return lax.psum(jnp.sum(gradient * gradient, 0), ("stn", "cell"))

    def adjoint(residual):
        gathered = full_rows(residual)
        pulled = jnp.einsum("nij,ik->njk", sens_blocks, gathered, precision=lax.Precision.HIGHEST)
        weighted = slope_cells * pulled
        contribution = jnp.einsum(
            "nib,nik->nbk", basis_table, weighted, precision=lax.Precision.HIGHEST
        )
        contribution = contribution.reshape(slot_count, -1, centre_count, members)
        grouped = jnp.einsum("noj,nobk->jbk", onehot, contribution, precision=lax.Precision.HIGHEST)
        return control_total(grouped.reshape(-1, members))

    tanh_phi = jnp.tanh(cell_field(group_rows(controls)))
    density = 0.5 * (1.0 + tanh_phi)
    slope_cells = 0.5 * (1.0 - tanh_phi * tanh_phi)
    predicted = station_part(density)
    residual = observed - station_sum(predicted)
    gradient = adjoint(residual)
    grad_norm = control_square(gradient)
    direction = gradient
    update = jnp.zeros_like(gradient)
    for iteration in range(ITERS):
        values = slope_cells * cell_field(group_rows(direction))
        image_vec = station_sum(station_part(values))
        curvature = lax.psum(jnp.sum(image_vec * image_vec, 0), ("stn", "cell"))
        step_size = grad_norm / curvature
        update = update + step_size * direction
        residual = residual - step_size * image_vec
        if iteration + 1 < ITERS:
            gradient = adjoint(residual)
            new_norm = control_square(gradient)
            direction = gradient + new_norm / grad_norm * direction
            grad_norm = new_norm
    return (controls + update, residual)


def solution(mesh):
    return jax.shard_map(
        local,
        mesh=mesh,
        in_specs=(
            P("stn", "cell", None, None, None),
            P("stn", "cell", None),
            P("cell", None),
            P("cell", None),
            P(("stn", "cell"), None),
            P(("stn", "cell"), None),
        ),
        out_specs=(P(("stn", "cell"), None), P(("stn", "cell"), None)),
        check_vma=False,
    )
```

profile of v0, /device:TPU:1, one launch (start us, length us, event | category | flops | bytes accessed | tf_op | source)
XLA Modules:
  0.0 1659.8 jit_solution(6081712787842085225)
XLA Ops:
  10.5 1.4 gather_fusion.1
  11.9 44.3 %all_gather.21 = f32[1024,128]{1,0:T(8,128)S(1)} all-gather(f32[32,128]{1,0:T(8,128)S(1)} %copy-done.7), channel_id=1, replica_groups=mesh['stn'=32,'cell'=16] {'stn'}, dimensions={0}, use_global_device_ids=true | all-gather | bytes 540672 | tf_op jit(solution)/shard_map/all_gather | solution.py:52
  58.0 1.2 convolution_bitcast_fusion.9
  60.1 65.6 %reduce-scatter.22.cloned.1.call-done = f32[32,128]{1,0:T(8,128)} async-done(((f32[512,128]{1,0:T(8,128)}), f32[32,128]{1,0:T(8,128)}) %reduce-scatter.22.cloned.1.call-update) | async-done | bytes 16400 | tf_op jit(solution)/shard_map/reduce_scatter | solution.py:58
  126.4 17.0 %all_gather.22 = f32[512,128]{1,0:T(8,128)S(1)} all-gather(f32[32,128]{1,0:T(8,128)S(1)} %sub.92), channel_id=1, replica_groups=mesh['stn'=32,'cell'=16] {'cell'}, dimensions={0}, use_global_device_ids=true | all-gather | bytes 278528 | tf_op jit(solution)/shard_map/all_gather | solution.py:61
  144.7 1.9 fusion.19
  148.2 212.9 %reduce-scatter.24.cloned.1.call-done = f32[32,128]{1,0:T(8,128)} async-done(((f32[1024,128]{1,0:T(8,128)}), f32[32,128]{1,0:T(8,128)}) %reduce-scatter.24.cloned.1.call-update) | async-done | bytes 16400 | tf_op jit(solution)/shard_map/reduce_scatter | solution.py:64
  361.2 36.5 %all_gather.23 = f32[1024,128]{1,0:T(8,128)S(1)} all-gather(f32[32,128]{1,0:T(8,128)} %reduce-scatter.24.cloned.1.call-done), channel_id=1, replica_groups=mesh['stn'=32,'cell'=16] {'stn'}, dimensions={0}, use_global_device_ids=true | all-gather | bytes 540672 | tf_op jit(solution)/shard_map/all_gather | solution.py:52
  402.3 70.5 %reduce-scatter.26.cloned.1.call-done = f32[32,128]{1,0:T(8,128)} async-done(((f32[512,128]{1,0:T(8,128)}), f32[32,128]{1,0:T(8,128)}) %reduce-scatter.26.cloned.1.call-update) | async-done | bytes 16400 | tf_op jit(solution)/shard_map/reduce_scatter | solution.py:58
  473.8 100.1 %all-reduce = (f32[128]{0:T(128)S(1)}, f32[128]{0:T(128)S(1)}) all-reduce(f32[128]{0:T(128)S(1)} %multiply_reduce_fusion.5, f32[128]{0:T(128)S(1)} %multiply_reduce_fusion.4), channel_id=1, replica_groups=mesh['stn'=32,'cell'=16] {'stn','cell'}, use_global_device_ids=true, to_apply=%region_3.4 | all-reduce | flops 256 | bytes 2048 | tf_op jit(solution)/shard_map/psum | solution.py:67
  573.9 16.8 %all_gather.24 = f32[512,128]{1,0:T(8,128)S(1)} all-gather(f32[32,128]{1,0:T(8,128)S(1)} %multiply_subtract_fusion.2), channel_id=1, replica_groups=mesh['stn'=32,'cell'=16] {'cell'}, dimensions={0}, use_global_device_ids=true | all-gather | bytes 278528 | tf_op jit(solution)/shard_map/all_gather | solution.py:61
  591.9 1.9 fusion.18
  595.5 210.3 %reduce-scatter.28.cloned.1.call-done = f32[32,128]{1,0:T(8,128)} async-done(((f32[1024,128]{1,0:T(8,128)}), f32[32,128]{1,0:T(8,128)}) %reduce-scatter.28.cloned.1.call-update) | async-done | bytes 16400 | tf_op jit(solution)/shard_map/reduce_scatter | solution.py:64
  806.7 100.5 %psum.44 = f32[128]{0:T(128)S(1)} all-reduce(f32[128]{0:T(128)S(1)} %multiply_reduce_fusion.3), channel_id=1, replica_groups=mesh['stn'=32,'cell'=16] {'stn','cell'}, use_global_device_ids=true, to_apply=%region_9.10 | all-reduce | flops 128 | bytes 1024 | tf_op jit(solution)/shard_map/psum | solution.py:67
  907.3 36.0 %all_gather.25 = f32[1024,128]{1,0:T(8,128)S(1)} all-gather(f32[32,128]{1,0:T(8,128)S(1)} %multiply_add_fusion.1), channel_id=1, replica_groups=mesh['stn'=32,'cell'=16] {'stn'}, dimensions={0}, use_global_device_ids=true | all-gather | bytes 540672 | tf_op jit(solution)/shard_map/all_gather | solution.py:52
  947.2 65.1 %reduce-scatter.30.cloned.1.call-done = f32[32,128]{1,0:T(8,128)} async-done(((f32[512,128]{1,0:T(8,128)}), f32[32,128]{1,0:T(8,128)}) %reduce-scatter.30.cloned.1.call-update) | async-done | bytes 16400 | tf_op jit(solution)/shard_map/reduce_scatter | solution.py:58
  1013.1 100.0 %psum.45 = f32[128]{0:T(128)S(1)} all-reduce(f32[128]{0:T(128)S(1)} %multiply_reduce_fusion.2), channel_id=1, replica_groups=mesh['stn'=32,'cell'=16] {'stn','cell'}, use_global_device_ids=true, to_apply=%region_12.13 | all-reduce | flops 128 | bytes 1024 | tf_op jit(solution)/shard_map/psum | solution.py:92
  1113.2 16.5 all_gather.26
  1130.9 1.9 fusion.17
  1134.5 210.4 %reduce-scatter.32.cloned.1.call-done = f32[32,128]{1,0:T(8,128)} async-done(((f32[1024,128]{1,0:T(8,128)}), f32[32,128]{1,0:T(8,128)}) %reduce-scatter.32.cloned.1.call-update) | async-done | bytes 16400 | tf_op jit(solution)/shard_map/reduce_scatter | solution.py:64
  1345.7 100.6 %psum.46 = f32[128]{0:T(128)S(1)} all-reduce(f32[128]{0:T(128)S(1)} %multiply_reduce_fusion.1), channel_id=1, replica_groups=mesh['stn'=32,'cell'=16] {'stn','cell'}, use_global_device_ids=true, to_apply=%region_15.16 | all-reduce | flops 128 | bytes 1024 | tf_op jit(solution)/shard_map/psum | solution.py:67
  1446.3 36.3 %all_gather.27 = f32[1024,128]{1,0:T(8,128)S(1)} all-gather(f32[32,128]{1,0:T(8,128)S(1)} %multiply_add_fusion), channel_id=1, replica_groups=mesh['stn'=32,'cell'=16] {'stn'}, dimensions={0}, use_global_device_ids=true | all-gather | bytes 540672 | tf_op jit(solution)/shard_map/all_gather | solution.py:52
  1486.4 65.3 %reduce-scatter.34.cloned.1.call-done = f32[32,128]{1,0:T(8,128)} async-done(((f32[512,128]{1,0:T(8,128)}), f32[32,128]{1,0:T(8,128)}) %reduce-scatter.34.cloned.1.call-update) | async-done | bytes 16400 | tf_op jit(solution)/shard_map/reduce_scatter | solution.py:58
  1552.6 99.8 %psum.47 = f32[128]{0:T(128)S(1)} all-reduce(f32[128]{0:T(128)S(1)} %multiply_reduce_fusion), channel_id=1, replica_groups=mesh['stn'=32,'cell'=16] {'stn','cell'}, use_global_device_ids=true, to_apply=%region_18.19 | all-reduce | flops 128 | bytes 1024 | tf_op jit(solution)/shard_map/psum | solution.py:92
  (102 shorter events, 32.7 us)
Async XLA Ops:
  7.2 50.8 %copy-start = (bf16[1,1,2,512,512]{4,3,2,1,0:T(8,128)(2,1)S(1)}, bf16[1,1,2,512,512]{4,3,2,1,0:T(8,128)(2,1)}, u32[]{:S(2)}) copy-start(bf16[1,1,2,512,512]{4,3,2,1,0:T(8,128)(2,1)} %param.6) | copy-start | bytes 3145732
  7.2 0.8 copy-start.11
  7.2 118.5 %reduce-scatter.22.cloned.1.call-start = ((), (), s32[]{:S(2)}) async-start(), calls=%async_computation.7 | async-start | bytes 278528 | tf_op jit(solution)/shard_map/reduce_scatter | solution.py:58
  8.0 0.7 copy-start.10
  9.8 0.7 copy-start.1
  10.5 1.4 copy-start.7
  60.0 65.7 %copy-start.9 = (f32[32,128]{1,0:T(8,128)S(1)}, f32[32,128]{1,0:T(8,128)}, u32[]{:S(2)}) copy-start(f32[32,128]{1,0:T(8,128)} %param.11) | copy-start | bytes 49156
  60.0 301.1 %reduce-scatter.24.cloned.1.call-start = ((), (), s32[]{:S(2)}) async-start(), calls=%async_computation.8 | async-start | bytes 540672 | tf_op jit(solution)/shard_map/reduce_scatter | solution.py:64
  148.2 324.7 %reduce-scatter.26.cloned.1.call-start = ((), (), s32[]{:S(2)}) async-start(), calls=%async_computation.9 | async-start | bytes 278528 | tf_op jit(solution)/shard_map/reduce_scatter | solution.py:58
  401.4 0.7 copy-start.2
  401.4 404.3 %reduce-scatter.28.cloned.1.call-start = ((), (), s32[]{:S(2)}) async-start(), calls=%async_computation.10 | async-start | bytes 540672 | tf_op jit(solution)/shard_map/reduce_scatter | solution.py:64
  473.7 100.2 %copy-start.4 = (f32[32,128]{1,0:T(8,128)S(1)}, f32[32,128]{1,0:T(8,128)}, u32[]{:S(2)}) copy-start(f32[32,128]{1,0:T(8,128)} %reduce-scatter.26.cloned.1.call-done) | copy-start | bytes 49156
  595.4 416.8 %reduce-scatter.30.cloned.1.call-start = ((), (), s32[]{:S(2)}) async-start(), calls=%async_computation.11 | async-start | bytes 278528 | tf_op jit(solution)/shard_map/reduce_scatter | solution.py:58
  806.6 100.7 %copy-start.6 = (f32[32,128]{1,0:T(8,128)S(1)}, f32[32,128]{1,0:T(8,128)}, u32[]{:S(2)}) copy-start(f32[32,128]{1,0:T(8,128)} %reduce-scatter.28.cloned.1.call-done) | copy-start | bytes 49156
  947.1 397.7 %reduce-scatter.32.cloned.1.call-start = ((), (), s32[]{:S(2)}) async-start(), calls=%async_computation.12 | async-start | bytes 540672 | tf_op jit(solution)/shard_map/reduce_scatter | solution.py:64
  1013.0 100.2 %copy-start.5 = (f32[32,128]{1,0:T(8,128)S(1)}, f32[32,128]{1,0:T(8,128)}, u32[]{:S(2)}) copy-start(f32[32,128]{1,0:T(8,128)} %reduce-scatter.30.cloned.1.call-done) | copy-start | bytes 49156
  1134.4 417.2 %reduce-scatter.34.cloned.1.call-start = ((), (), s32[]{:S(2)}) async-start(), calls=%async_computation.13 | async-start | bytes 278528 | tf_op jit(solution)/shard_map/reduce_scatter | solution.py:58
  1345.6 100.7 %copy-start.3 = (f32[32,128]{1,0:T(8,128)S(1)}, f32[32,128]{1,0:T(8,128)}, u32[]{:S(2)}) copy-start(f32[32,128]{1,0:T(8,128)} %reduce-scatter.32.cloned.1.call-done) | copy-start | bytes 49156
  1552.4 99.9 %copy-start.8 = (f32[32,128]{1,0:T(8,128)S(1)}, f32[32,128]{1,0:T(8,128)}, u32[]{:S(2)}) copy-start(f32[32,128]{1,0:T(8,128)} %reduce-scatter.34.cloned.1.call-done) | copy-start | bytes 49156
Sparse Core Ops, SparseCore 0:
  60.2 65.5 reduce-scatter.21
  148.3 212.8 reduce-scatter.23
  401.6 71.2 reduce-scatter.25
  595.5 210.2 reduce-scatter.27
  947.2 64.9 reduce-scatter.29
  1134.5 210.2 reduce-scatter.31
  1486.5 65.0 reduce-scatter.33
where the time goes:
time: 1660 us
  waiting for transfers between devices  900 us (54%)
  blocking collectives  704 us (42%)
  matrix products  20.2 us (1%)
  local copies, waits for them, and re-layouts  17.3 us (1%)
    reduce_scatter x3, waiting for transfers between devices, control_total(): return lax.psum_scatter(grouped, 'stn', scatter_dimension=0, tiled=True)  634 us
    psum x3, blocking collectives, control_square(): return lax.psum(jnp.sum(gradient * gradient, 0), ('stn', 'cell'))  301 us
    reduce_scatter x4, waiting for transfers between devices, station_sum(): lax.psum_scatter(partial_rows, 'cell', scatter_dimension=0, tiled=True)  266 us
    psum x2, blocking collectives, local(): curvature = lax.psum(jnp.sum(image_vec * image_vec, 0), ('stn', 'cell'))  200 us
    all_gather x4, blocking collectives, group_rows(): return lax.all_gather(vector, 'stn', axis=0, tiled=True)  153 us
    all_gather x3, blocking collectives, full_rows(): return lax.all_gather(residual, 'cell', axis=0, tiled=True)  50.3 us
  transfers between devices with their start and end apart: 7, of which 7 were waited for; matrix products, arithmetic and copies ran while one was open for 0% of the time, Pallas kernels for 0%

commit v1 on v0

v1 whole, which is shorter than its diff:
```python
import jax
import jax.numpy as jnp
from jax import lax
from jax.experimental import pallas as pl
from jax.experimental.pallas import tpu as pltpu
from jax.sharding import PartitionSpec as P

MESH = pl.DeviceIdType.MESH
ITERS = 3
SLOTS, BLOCK, MARGINS, CENTRES, MEMBERS = 2, 512, 4, 32, 128
NX, NZ, NY = 4, 8, 8
NSTN, NCELL = NX * NZ, NY * 2
F32, BF16 = jnp.float32, jnp.bfloat16


def split(value):
    high = value.astype(BF16)
    low = (value - high.astype(F32)).astype(BF16)
    return high, low


def column_sum(value):
    return jnp.sum(value.reshape(-1, MEMBERS), axis=0, keepdims=True)


def kernel(
    sens_hbm, blocks, margin, centres, controls, observed, updated, final_residual,
    sens, sens_t, basis, basis_t, coeff_rhs, cell_rhs, row_rhs, slope,
    gath, part, core_in, paired, y_in, full, grouped, x_in, x_sum, z_in,
    own_grad, own_dir, own_image, own_res, own_upd,
    row_core, row_core_in, row_y, row_y_in, row_x, row_x_in, row_z, row_z_in,
    sens_sem, gz_s, gz_r, gx_s, gx_r, c_s, c_r, y_s, y_r, fy_s, fy_r, fc_s, fc_r, dx_s, dx_r, dz_s, dz_r,
    rc_s, rc_r, ry_s, ry_r, rx_s, rx_r, rz_s, rz_r,
):
    stn, cell = lax.axis_index("stn"), lax.axis_index("cell")
    x, z = stn // NZ, stn % NZ
    y, core = cell // 2, cell % 2
    x_peers = [((x + d) % NX, ((x + d) % NX) * NZ + z, cell) for d in range(1, NX)]
    z_peers = [((z + d) % NZ, x * NZ + (z + d) % NZ, cell) for d in range(1, NZ)]
    y_peers = [((y + d) % NY, stn, ((y + d) % NY) * 2 + core) for d in range(1, NY)]
    core_peer = (1 - core, stn, y * 2 + 1 - core)

    def send(src, dst, ssem, rsem, peer):
        pltpu.make_async_remote_copy(
            src_ref=src, dst_ref=dst, send_sem=ssem, recv_sem=rsem,
            device_id={"stn": peer[1], "cell": peer[2]}, device_id_type=MESH,
        ).start()

    def drain(ref, sem):
        pltpu.make_async_copy(ref, ref, sem).wait()

    barrier = pltpu.get_barrier_semaphore()
    everyone = x_peers + z_peers + y_peers + [core_peer]
    for peer in everyone:
        pl.semaphore_signal(
            barrier, inc=1, device_id={"stn": peer[1], "cell": peer[2]}, device_id_type=MESH
        )
    load = pltpu.make_async_copy(sens_hbm, sens, sens_sem)
    load.start()
    gath[0, stn] = controls[...]
    pl.semaphore_wait(barrier, len(everyone))

    def gather_z(k):
        for peer in z_peers:
            send(gath.at[k, stn], gath.at[k, stn], gz_s.at[k], gz_r.at[k], peer)

    def gather_x(k):
        drain(gath.at[k, 0:NZ - 1], gz_r.at[k])
        rows = pl.ds(x * NZ, NZ)
        for peer in x_peers:
            send(gath.at[k, rows], gath.at[k, rows], gx_s.at[k], gx_r.at[k], peer)

    def gather_end(k):
        drain(gath.at[k, 0:NSTN - NZ], gx_r.at[k])

    gather_z(0)

    lane = lax.broadcasted_iota(jnp.int32, (8, MEMBERS), 1)
    rows_of_centres = [
        jnp.broadcast_to(centres[0:1, i * MEMBERS:(i + 1) * MEMBERS], (8, MEMBERS)) for i in range(8)
    ]
    listed = []
    for n in range(SLOTS):
        block = blocks[n]
        listed.append([margin[block, o] for o in range(MARGINS)])
        centre = jnp.zeros((8, MEMBERS), jnp.int32)
        for o in range(MARGINS):
            j = listed[n][o]
            row = rows_of_centres[0]
            for i in range(1, 8):
                row = jnp.where(j // 4 == i, rows_of_centres[i], row)
            turned = row
            for i in range(1, 4):
                turned = jnp.where((o + 4 - j % 4) % 4 == i, pltpu.roll(row, i * CENTRES, 1), turned)
            centre = jnp.where(lane // CENTRES == o, turned, centre)
        centre = centre[0:1]
        cells = lax.broadcasted_iota(jnp.int32, (BLOCK, MEMBERS), 0) + block * BLOCK
        squared = jnp.zeros((BLOCK, MEMBERS), F32)
        for shift, mask in ((10, 1048575), (5, 31), (0, 31)):
            cell_coord = ((cells >> shift) & mask).astype(F32)
            centre_coord = ((centre >> shift) & mask).astype(F32)
            spread = cell_coord - centre_coord
            squared = squared + spread * spread
        table = jnp.exp(squared * (-0.5 / 100.0))
        high, low = split(table)
        basis[n, :, 0:MEMBERS] = high
        basis[n, :, MEMBERS:] = low
        high, low = split(table.T)
        basis_t[n, 0:MEMBERS] = high
        basis_t[n, MEMBERS:] = low

    gather_x(0)
    load.wait()
    for n in range(SLOTS):
        for i in range(4):
            piece = sens[n, i * 128:(i + 1) * 128, :]
            sens_t[n, :, i * 128:(i + 1) * 128] = piece.T
    gather_end(0)

    def field(k, n):
        for o in range(MARGINS):
            high, low = split(gath[k, listed[n][o]])
            for base in (0, MEMBERS):
                at = slice(base + o * CENTRES, base + (o + 1) * CENTRES)
                coeff_rhs[n, at, 0:MEMBERS] = high
                coeff_rhs[n, at, MEMBERS:] = low
        both = jnp.dot(basis[n], coeff_rhs[n], preferred_element_type=F32)
        return both[:, 0:MEMBERS] + both[:, MEMBERS:]

    def station(k):
        both = jnp.dot(sens[0], cell_rhs[0], preferred_element_type=F32)
        both += jnp.dot(sens[1], cell_rhs[1], preferred_element_type=F32)
        part[k] = (both[:, 0:MEMBERS] + both[:, MEMBERS:]).reshape(NCELL // 2, 2, CENTRES, MEMBERS)

    def put_cells(n, value):
        high, low = split(value)
        cell_rhs[n, :, 0:MEMBERS] = high
        cell_rhs[n, :, MEMBERS:] = low

    def sum_cells(k, with_norm):
        send(part.at[k, :, 1 - core], core_in.at[k], c_s.at[k], c_r.at[k], core_peer)
        drain(core_in.at[k], c_r.at[k])
        paired[k] = part[k, :, core] + core_in[k]
        for peer in y_peers:
            send(paired.at[k, peer[0]], y_in.at[k, y], y_s.at[k], y_r.at[k], peer)
        y_in[k, y] = paired[k, y]
        norm = None
        if with_norm:
            drain(row_core_in.at[k], rc_r.at[k])
            row_y[k] = row_core[k] + row_core_in[k]
            for peer in y_peers:
                send(row_y.at[k], row_y_in.at[k, y], ry_s.at[k], ry_r.at[k], peer)
            row_y_in[k, y] = row_y[k]
            drain(row_y_in.at[k, 0:NY - 1], ry_r.at[k])
            norm = sum(row_y_in[k, i] for i in range(NY))
        drain(y_in.at[k, 0:NY - 1], y_r.at[k])
        return sum(y_in[k, i] for i in range(NY)), norm

    def gather_cells(k, rows):
        full[k, y, core] = rows
        for peer in y_peers:
            send(full.at[k, y, core], full.at[k, y, core], fy_s.at[k], fy_r.at[k], peer)
        drain(full.at[k, 0:NY - 1, 0], fy_r.at[k])
        send(full.at[k, :, core], full.at[k, :, core], fc_s.at[k], fc_r.at[k], core_peer)
        drain(full.at[k, :, 0], fc_r.at[k])

    def adjoint(k, with_curvature):
        rows = full[k].reshape(BLOCK, MEMBERS)
        if with_curvature:
            row_x[k] = column_sum(rows * rows)
            for peer in x_peers:
                send(row_x.at[k], row_x_in.at[k, x], rx_s.at[k], rx_r.at[k], peer)
            row_x_in[k, x] = row_x[k]
        high, low = split(rows)
        row_rhs[:, 0:MEMBERS] = high
        row_rhs[:, MEMBERS:] = low
        parts = []
        for n in range(SLOTS):
            pulled = jnp.dot(sens_t[n], row_rhs[...], preferred_element_type=F32)
            put_cells(n, slope[n] * (pulled[:, 0:MEMBERS] + pulled[:, MEMBERS:]))
            four = jnp.dot(basis_t[n], cell_rhs[n], preferred_element_type=F32)
            two = four[:, 0:MEMBERS] + four[:, MEMBERS:]
            parts.append((two[0:MEMBERS] + two[MEMBERS:]).reshape(MARGINS, CENTRES, MEMBERS))
        for j in range(NSTN):
            total = None
            for n in range(SLOTS):
                for o in range(MARGINS):
                    term = jnp.where(listed[n][o] == j, parts[n][o], 0.0)
                    total = term if total is None else total + term
            grouped[k, j // NZ, j % NZ] = total
        for peer in x_peers:
            send(grouped.at[k, peer[0]], x_in.at[k, x], dx_s.at[k], dx_r.at[k], peer)
        x_in[k, x] = grouped[k, x]
        drain(x_in.at[k, 0:NX - 1], dx_r.at[k])
        x_sum[k] = sum(x_in[k, i] for i in range(NX))
        for peer in z_peers:
            send(x_sum.at[k, peer[0]], z_in.at[k, z], dz_s.at[k], dz_r.at[k], peer)
        z_in[k, z] = x_sum[k, z]
        curvature = None
        if with_curvature:
            drain(row_x_in.at[k, 0:NX - 1], rx_r.at[k])
            row_z[k] = sum(row_x_in[k, i] for i in range(NX))
            for peer in z_peers:
                send(row_z.at[k], row_z_in.at[k, z], rz_s.at[k], rz_r.at[k], peer)
            row_z_in[k, z] = row_z[k]
            drain(row_z_in.at[k, 0:NZ - 1], rz_r.at[k])
            curvature = sum(row_z_in[k, i] for i in range(NZ))
        drain(z_in.at[k, 0:NZ - 1], dz_r.at[k])
        return sum(z_in[k, i] for i in range(NZ)), curvature

    for n in range(SLOTS):
        tanh_phi = jnp.tanh(field(0, n))
        slope[n] = 0.5 * (1.0 - tanh_phi * tanh_phi)
        put_cells(n, 0.5 * (1.0 + tanh_phi))
    station(0)
    predicted, _ = sum_cells(0, False)
    own_res[...] = observed[...] - predicted
    gather_cells(0, own_res[...])
    gradient, _ = adjoint(0, False)
    own_grad[...] = gradient

    norm = None
    for k in range(1, ITERS + 1):
        gath[k, stn] = own_grad[...]
        gather_z(k)
        gather_x(k)
        gather_end(k)
        row_core[k] = column_sum(gath[k] * gath[k])
        send(row_core.at[k], row_core_in.at[k], rc_s.at[k], rc_r.at[k], core_peer)
        for n in range(SLOTS):
            put_cells(n, slope[n] * field(k, n))
        station(k)
        image, new_norm = sum_cells(k, True)
        direction = own_grad[...]
        if k > 1:
            ratio = new_norm / norm
            image = image + ratio * own_image[...]
            direction = direction + ratio * own_dir[...]
        norm = new_norm
        own_image[...] = image
        own_dir[...] = direction
        if k < ITERS:
            gather_cells(k, image)
            change, curvature = adjoint(k, True)
            step = norm / curvature
            own_grad[...] = own_grad[...] - step * change
        else:
            row_core[0] = column_sum(image * image)
            send(row_core.at[0], row_core_in.at[0], rc_s.at[0], rc_r.at[0], core_peer)
            drain(row_core_in.at[0], rc_r.at[0])
            row_y[0] = row_core[0] + row_core_in[0]
            for peer in y_peers:
                send(row_y.at[0], row_y_in.at[0, y], ry_s.at[0], ry_r.at[0], peer)
            row_y_in[0, y] = row_y[0]
            drain(row_y_in.at[0, 0:NY - 1], ry_r.at[0])
            row_x[0] = sum(row_y_in[0, i] for i in range(NY))
            for peer in x_peers:
                send(row_x.at[0], row_x_in.at[0, x], rx_s.at[0], rx_r.at[0], peer)
            row_x_in[0, x] = row_x[0]
            drain(row_x_in.at[0, 0:NX - 1], rx_r.at[0])
            row_z[0] = sum(row_x_in[0, i] for i in range(NX))
            for peer in z_peers:
                send(row_z.at[0], row_z_in.at[0, z], rz_s.at[0], rz_r.at[0], peer)
            row_z_in[0, z] = row_z[0]
            drain(row_z_in.at[0, 0:NZ - 1], rz_r.at[0])
            step = norm / sum(row_z_in[0, i] for i in range(NZ))
        own_res[...] = own_res[...] - step * image
        own_upd[...] = step * direction if k == 1 else own_upd[...] + step * direction

    updated[...] = controls[...] + own_upd[...]
    final_residual[...] = own_res[...]

    for k in range(ITERS + 1):
        drain(gath.at[k, 0:NZ - 1], gz_s.at[k])
        drain(gath.at[k, 0:NSTN - NZ], gx_s.at[k])
        drain(core_in.at[k], c_s.at[k])
        drain(y_in.at[k, 0:NY - 1], y_s.at[k])
        drain(row_core_in.at[k], rc_s.at[k])
        drain(row_y_in.at[k, 0:NY - 1], ry_s.at[k])
    for k in range(ITERS):
        drain(full.at[k, 0:NY - 1, 0], fy_s.at[k])
        drain(full.at[k, :, 0], fc_s.at[k])
        drain(x_in.at[k, 0:NX - 1], dx_s.at[k])
        drain(z_in.at[k, 0:NZ - 1], dz_s.at[k])
        drain(row_x_in.at[k, 0:NX - 1], rx_s.at[k])
        drain(row_z_in.at[k, 0:NZ - 1], rz_s.at[k])


def local(sensitivity, block_list, margin, centres, controls, observed):
    rows = (CENTRES, MEMBERS)
    a, d = ITERS + 1, ITERS

    def vmem(*shape):
        return pltpu.VMEM(shape, F32)

    scratch = [
        pltpu.VMEM((SLOTS, BLOCK, BLOCK), BF16),
        pltpu.VMEM((SLOTS, BLOCK, BLOCK), BF16),
        pltpu.VMEM((SLOTS, BLOCK, 2 * MEMBERS), BF16),
        pltpu.VMEM((SLOTS, 2 * MEMBERS, BLOCK), BF16),
        pltpu.VMEM((SLOTS, 2 * MEMBERS, 2 * MEMBERS), BF16),
        pltpu.VMEM((SLOTS, BLOCK, 2 * MEMBERS), BF16),
        pltpu.VMEM((BLOCK, 2 * MEMBERS), BF16),
        vmem(SLOTS, BLOCK, MEMBERS),
        vmem(a, NSTN, *rows),
        vmem(a, NY, 2, *rows),
        vmem(a, NY, *rows),
        vmem(a, NY, *rows),
        vmem(a, NY, *rows),
        vmem(d, NY, 2, *rows),
        vmem(d, NX, NZ, *rows),
        vmem(d, NX, NZ, *rows),
        vmem(d, NZ, *rows),
        vmem(d, NZ, *rows),
        vmem(*rows), vmem(*rows), vmem(*rows), vmem(*rows), vmem(*rows),
        vmem(a, 1, MEMBERS), vmem(a, 1, MEMBERS),
        vmem(a, 1, MEMBERS), vmem(a, NY, 1, MEMBERS),
        vmem(d, 1, MEMBERS), vmem(d, NX, 1, MEMBERS),
        vmem(d, 1, MEMBERS), vmem(d, NZ, 1, MEMBERS),
        pltpu.SemaphoreType.DMA,
    ]
    scratch += [pltpu.SemaphoreType.DMA((a,))] * 8
    scratch += [pltpu.SemaphoreType.DMA((d,))] * 8
    scratch += [pltpu.SemaphoreType.DMA((a,))] * 4
    scratch += [pltpu.SemaphoreType.DMA((d,))] * 4
    in_vmem = pl.BlockSpec(memory_space=pltpu.VMEM)
    in_smem = pl.BlockSpec(memory_space=pltpu.SMEM)
    return pl.pallas_call(
        kernel,
        out_shape=(jax.ShapeDtypeStruct(rows, F32), jax.ShapeDtypeStruct(rows, F32)),
        in_specs=[pl.BlockSpec(memory_space=pl.ANY), in_smem, in_smem, in_vmem, in_vmem, in_vmem],
        out_specs=(in_vmem, in_vmem),
        scratch_shapes=scratch,
        compiler_params=pltpu.CompilerParams(
            collective_id=0, has_side_effects=True, vmem_limit_bytes=40 * 1024 * 1024
        ),
        cost_estimate=pl.CostEstimate(flops=3_000_000_000, bytes_accessed=2_000_000, transcendentals=262144),
        name="gauss_newton",
    )(
        sensitivity.reshape(SLOTS, BLOCK, BLOCK), block_list.reshape(SLOTS), margin, centres,
        controls, observed,
    )


def solution(mesh):
    return jax.shard_map(
        local,
        mesh=mesh,
        in_specs=(
            P("stn", "cell", None, None, None),
            P("stn", "cell", None),
            P("cell", None),
            P("cell", None),
            P(("stn", "cell"), None),
            P(("stn", "cell"), None),
        ),
        out_specs=(P(("stn", "cell"), None), P(("stn", "cell"), None)),
        check_vma=False,
    )
```

time: 1660 us -> 188 us (0.11)
  waiting for transfers between devices: 900 us -> 0 us
  blocking collectives: 704 us -> 0 us
  Pallas kernels: 0 us -> 182 us
  matrix products: 20.2 us -> 0 us
    reduce_scatter x7 -> x0, waiting for transfers between devices: 900 us -> none  [the longest x3 634 us: control_total(): return lax.psum_scatter(grouped, 'stn', scatter_dimension=0, tiled=True)]
    psum x5 -> x0, blocking collectives: 501 us -> none  [the longest x3 301 us: control_square(): return lax.psum(jnp.sum(gradient * gradient, 0), ('stn', 'cell'))]
    all_gather x7 -> x0, blocking collectives: 203 us -> none  [the longest x4 153 us: group_rows(): return lax.all_gather(vector, 'stn', axis=0, tiled=True)]
    pallas_call x0 -> x1, Pallas kernels: none -> 182 us  [local(): pl.pallas_call(kernel, out_shape=(jax.ShapeDtypeStruct(rows, F32), jax.Sh...]
    dot_general x17 -> x0, matrix products: 20.2 us -> none  [the longest x3 5.56 us: adjoint(): jnp.einsum('nib,nik->nbk', basis_table, weighted, precision=lax.Precision...]
  transfers between devices with their start and end apart: 7 -> 0, of which waited for: 7 -> 0; matrix products, arithmetic and copies ran while one was open for 0% -> 0% of each run, Pallas kernels for 0% -> 0%
where the time goes in v1:
time: 188 us; the launch traced here: 186 us
  Pallas kernels  182 us (97%)
  local copies, waits for them, and re-layouts  3.24 us (2%)
    pallas_call x1, Pallas kernels, local(): pl.pallas_call(kernel, out_shape=(jax.ShapeDtypeStruct(rows, F32), jax.Sh...  182 us

profile of v1, /device:TPU:1, one launch (start us, length us, event | category | flops | bytes accessed | tf_op | source)
XLA Modules:
  0.0 186.1 jit_solution(5088552379244541123)
XLA Ops:
  0.6 0.0 copy-start.3
  0.6 0.0 copy-start.1
  0.7 0.0 copy-start.2
  0.7 0.0 copy-start.4
  0.7 0.8 copy.8.margin
  1.5 0.0 copy-done.3
  1.5 0.0 copy-done.1
  1.5 0.0 copy-done.2
  1.5 0.0 copy-done.4
  1.5 0.0 copy-start
  1.5 1.2 copy-done
  2.7 182.1 %gauss_newton.1 = (f32[32,128]{1,0:T(8,128)S(1)}, f32[32,128]{1,0:T(8,128)S(1)}) custom-call(bf16[2,512,512]{2,1,0:T(8,128)(2,1)S(1)} %bitcast.2, s32[2]{0:T(128)S(1)} %bitcast.3, s32[64,4]{1,0:T(8,128)S(1)} %copy.8.margin, s32[1,1024]{1,0:T(1,128)S(1)} %copy-done.3, f32[32,128]{1,0:T(8,128)S(1)} %copy-done.1, f32[32,128]{1,0:T(8,128)S(1)} %copy-done.2), custom_call_target="tpu_custom_call" | custom-call | flops 3000000000 | bytes 2000000 | tf_op jit(solution)/shard_map/gauss_newton/pallas_call | solution.py:328
  184.9 0.6 copy.11
  185.5 0.6 copy.12
Async XLA Ops:
  0.6 0.8 copy-start.3
  0.6 0.8 copy-start.1
  0.7 0.8 copy-start.2
  0.7 0.8 copy-start.4
  1.5 1.2 copy-start

commit v2 on v1

v2 whole, which is shorter than its diff:
```python
import jax
import jax.numpy as jnp
from jax import lax
from jax.experimental import pallas as pl
from jax.experimental.pallas import tpu as pltpu
from jax.sharding import PartitionSpec as P

MESH = pl.DeviceIdType.MESH
ITERS = 3
SLOTS, BLOCK, MARGINS, CENTRES, MEMBERS = 2, 512, 4, 32, 128
NX, NZ, NY = 4, 8, 8
NSTN, NCELL = NX * NZ, NY * 2
F32, BF16 = jnp.float32, jnp.bfloat16


def split(value):
    high = value.astype(BF16)
    low = (value - high.astype(F32)).astype(BF16)
    return high, low


def column_sum(value):
    return jnp.sum(value.reshape(-1, MEMBERS), axis=0, keepdims=True)


def interleave(first, second):
    upper = lax.broadcasted_iota(jnp.int32, first.shape, 1) < MARGINS
    even = jnp.where(upper, first, pltpu.roll(second, MARGINS, 1))
    odd = jnp.where(upper, pltpu.roll(first, MARGINS, 1), second)
    return even, odd


def kernel(
    sens_hbm, blocks, margin, centres, controls, observed, updated, final_residual,
    sens, sens_t, basis, basis_r, basis_t, coeff_rhs, cell_rhs, row_rhs, slope,
    list_in, hot, hot_t, grad_rhs, entry_rhs,
    gath, part, core_in, paired, y_in, full, scat_out, scat_in, ans_out, ans_in,
    own_grad, own_dir, own_image, own_res, own_upd,
    row_core, row_core_in, row_y, row_y_in, row_s, row_s_in, pair_out, pair_in,
    sens_sem, li_s, li_r, gz_s, gz_r, gx_s, gx_r, c_s, c_r, y_s, y_r, fy_s, fy_r, fc_s, fc_r,
    sc_s, sc_r, an_s, an_r, rc_s, rc_r, ry_s, ry_r, rs_s, rs_r, pr_s, pr_r,
):
    stn, cell = lax.axis_index("stn"), lax.axis_index("cell")
    x, z = stn // NZ, stn % NZ
    y, core = cell // 2, cell % 2
    x_peers = [((x + d) % NX, ((x + d) % NX) * NZ + z, cell) for d in range(1, NX)]
    z_peers = [((z + d) % NZ, x * NZ + (z + d) % NZ, cell) for d in range(1, NZ)]
    y_peers = [((y + d) % NY, stn, ((y + d) % NY) * 2 + core) for d in range(1, NY)]
    core_peer = (1 - core, stn, y * 2 + 1 - core)
    s_peers = [((stn + d) % NSTN, (stn + d) % NSTN, cell) for d in range(1, NSTN)]

    def send(src, dst, ssem, rsem, peer):
        pltpu.make_async_remote_copy(
            src_ref=src, dst_ref=dst, send_sem=ssem, recv_sem=rsem,
            device_id={"stn": peer[1], "cell": peer[2]}, device_id_type=MESH,
        ).start()

    def drain(ref, sem):
        pltpu.make_async_copy(ref, ref, sem).wait()

    barrier = pltpu.get_barrier_semaphore()
    everyone = s_peers + y_peers + [core_peer]
    for peer in everyone:
        pl.semaphore_signal(
            barrier, inc=1, device_id={"stn": peer[1], "cell": peer[2]}, device_id_type=MESH
        )
    load = pltpu.make_async_copy(sens_hbm, sens, sens_sem)
    load.start()
    gath[stn] = controls[...]
    pl.semaphore_wait(barrier, len(everyone))

    listed = [[margin[blocks[n], o] for o in range(MARGINS)] for n in range(SLOTS)]
    entry = lax.broadcasted_iota(jnp.int32, (SLOTS * MARGINS, MEMBERS), 0)
    lists = jnp.zeros((SLOTS * MARGINS, MEMBERS), F32)
    for n in range(SLOTS):
        for o in range(MARGINS):
            lists = jnp.where(entry == n * MARGINS + o, listed[n][o].astype(F32), lists)
    list_in[stn] = lists

    for peer in z_peers:
        send(gath.at[stn], gath.at[stn], gz_s, gz_r, peer)
    for peer in s_peers:
        send(list_in.at[stn], list_in.at[stn], li_s, li_r, peer)

    lane = lax.broadcasted_iota(jnp.int32, (8, MEMBERS), 1)
    rows_of_centres = [
        jnp.broadcast_to(centres[0:1, i * MEMBERS:(i + 1) * MEMBERS], (8, MEMBERS)) for i in range(8)
    ]
    to_row = lax.broadcasted_iota(jnp.int32, (MEMBERS, MEMBERS), 0)
    to_col = lax.broadcasted_iota(jnp.int32, (MEMBERS, MEMBERS), 1)
    by_row = (to_row == (to_col % MARGINS) * CENTRES + to_col // MARGINS).astype(BF16)
    for n in range(SLOTS):
        block = blocks[n]
        centre = jnp.zeros((8, MEMBERS), jnp.int32)
        for o in range(MARGINS):
            j = listed[n][o]
            row = rows_of_centres[0]
            for i in range(1, 8):
                row = jnp.where(j // 4 == i, rows_of_centres[i], row)
            turned = row
            for i in range(1, 4):
                turned = jnp.where((o + 4 - j % 4) % 4 == i, pltpu.roll(row, i * CENTRES, 1), turned)
            centre = jnp.where(lane // CENTRES == o, turned, centre)
        centre = centre[0:1]
        cells = lax.broadcasted_iota(jnp.int32, (BLOCK, MEMBERS), 0) + block * BLOCK
        squared = jnp.zeros((BLOCK, MEMBERS), F32)
        for shift, mask in ((10, 1048575), (5, 31), (0, 31)):
            cell_coord = ((cells >> shift) & mask).astype(F32)
            centre_coord = ((centre >> shift) & mask).astype(F32)
            spread = cell_coord - centre_coord
            squared = squared + spread * spread
        table = jnp.exp(squared * (-0.5 / 100.0))
        high, low = split(table)
        basis[n, :, 0:MEMBERS] = high
        basis[n, :, MEMBERS:] = low
        high = jnp.dot(high, by_row, preferred_element_type=F32)
        low = jnp.dot(low, by_row, preferred_element_type=F32)
        basis_r[n, :, 0:MEMBERS] = high.astype(BF16)
        basis_r[n, :, MEMBERS:] = low.astype(BF16)
        basis_t[n, 0:MEMBERS] = high.T.astype(BF16)
        basis_t[n, MEMBERS:] = low.T.astype(BF16)

    drain(gath.at[0:NZ - 1], gz_r)
    x_rows = pl.ds(x * NZ, NZ)
    for peer in x_peers:
        send(gath.at[x_rows], gath.at[x_rows], gx_s, gx_r, peer)
    load.wait()
    for n in range(SLOTS):
        for i in range(4):
            piece = sens[n, i * 128:(i + 1) * 128, :]
            sens_t[n, :, i * 128:(i + 1) * 128] = piece.T
    drain(list_in.at[0:NSTN - 1], li_r)
    flat_lists = list_in[...].reshape(NSTN * SLOTS * MARGINS, MEMBERS)
    found = (flat_lists == lax.broadcasted_iota(jnp.int32, flat_lists.shape, 1).astype(F32)).astype(F32)
    hot[...] = found.astype(BF16)
    hot_t[...] = found.T[0:NSTN].astype(BF16)
    grad_rhs[...] = jnp.zeros_like(grad_rhs)
    drain(gath.at[0:NSTN - NZ], gx_r)

    def times_basis(table, n):
        both = jnp.dot(table[n], coeff_rhs[n], preferred_element_type=F32)
        return both[:, 0:MEMBERS] + both[:, MEMBERS:]

    def put_coeffs(n, at, rows, value):
        high, low = split(value)
        for base in (0, MEMBERS):
            coeff_rhs[n, base + at:base + at + rows, 0:MEMBERS] = high
            coeff_rhs[n, base + at:base + at + rows, MEMBERS:] = low

    def both_ways(left, rhs):
        both = jnp.dot(left, rhs, preferred_element_type=F32)
        return both[:, 0:MEMBERS] + both[:, MEMBERS:]

    def station(k):
        both = jnp.dot(sens[0], cell_rhs[0], preferred_element_type=F32)
        both += jnp.dot(sens[1], cell_rhs[1], preferred_element_type=F32)
        part[k] = (both[:, 0:MEMBERS] + both[:, MEMBERS:]).reshape(NCELL // 2, 2, CENTRES, MEMBERS)

    def put_cells(n, value):
        high, low = split(value)
        cell_rhs[n, :, 0:MEMBERS] = high
        cell_rhs[n, :, MEMBERS:] = low

    def sum_cells(k, group_norm=None):
        send(part.at[k, :, 1 - core], core_in.at[k], c_s.at[k], c_r.at[k], core_peer)
        if group_norm is not None:
            row_core[k] = group_norm()
            send(row_core.at[k], row_core_in.at[k], rc_s.at[k], rc_r.at[k], core_peer)
        drain(core_in.at[k], c_r.at[k])
        paired[k] = part[k, :, core] + core_in[k]
        for peer in y_peers:
            send(paired.at[k, peer[0]], y_in.at[k, y], y_s.at[k], y_r.at[k], peer)
        y_in[k, y] = paired[k, y]
        norm = None
        if group_norm is not None:
            drain(row_core_in.at[k], rc_r.at[k])
            row_y[k] = row_core[k] + row_core_in[k]
            for peer in y_peers:
                send(row_y.at[k], row_y_in.at[k, y], ry_s.at[k], ry_r.at[k], peer)
            row_y_in[k, y] = row_y[k]
            drain(row_y_in.at[k, 0:NY - 1], ry_r.at[k])
            norm = sum(row_y_in[k, i] for i in range(NY))
        drain(y_in.at[k, 0:NY - 1], y_r.at[k])
        return sum(y_in[k, i] for i in range(NY)), norm

    def gather_cells(k, rows):
        full[k, y, core] = rows
        for peer in y_peers:
            send(full.at[k, y, core], full.at[k, y, core], fy_s.at[k], fy_r.at[k], peer)
        drain(full.at[k, 0:NY - 1, 0], fy_r.at[k])
        send(full.at[k, :, core], full.at[k, :, core], fc_s.at[k], fc_r.at[k], core_peer)
        drain(full.at[k, :, 0], fc_r.at[k])

    def adjoint(k, with_curvature):
        rows = full[k].reshape(BLOCK, MEMBERS)
        if with_curvature:
            row_s[k] = column_sum(rows * rows)
            for peer in s_peers:
                send(row_s.at[k], row_s_in.at[k, stn], rs_s.at[k], rs_r.at[k], peer)
            row_s_in[k, stn] = row_s[k]
        high, low = split(rows)
        row_rhs[:, 0:MEMBERS] = high
        row_rhs[:, MEMBERS:] = low
        parts = []
        for n in range(SLOTS):
            put_cells(n, slope[n] * both_ways(sens_t[n], row_rhs[...]))
            two = both_ways(basis_t[n], cell_rhs[n])
            parts.append((two[0:MEMBERS] + two[MEMBERS:]).reshape(CENTRES // 2, 2 * MARGINS, MEMBERS))
        even, odd = interleave(parts[0], parts[1])
        scat_out[k, :, 0] = even
        scat_out[k, :, 1] = odd
        for peer in s_peers:
            send(scat_out.at[k, peer[0] // 2, peer[0] % 2], scat_in.at[k, stn], sc_s.at[k], sc_r.at[k], peer)
        scat_in[k, stn] = scat_out[k, stn // 2, stn % 2]
        curvature = None
        if with_curvature:
            drain(row_s_in.at[k, 0:NSTN - 1], rs_r.at[k])
            curvature = sum(row_s_in[k, i] for i in range(NSTN))
        drain(scat_in.at[k, 0:NSTN - 1], sc_r.at[k])
        high, low = split(scat_in[k].reshape(NSTN * SLOTS * MARGINS, MEMBERS))
        entry_rhs[:, 0:MEMBERS] = high
        entry_rhs[:, MEMBERS:] = low
        return both_ways(hot_t[...], entry_rhs[...]), curvature

    def answer(k):
        high, low = split(own_grad[...])
        grad_rhs[0:NSTN, 0:MEMBERS] = high
        grad_rhs[0:NSTN, MEMBERS:] = low
        ans_out[k] = both_ways(hot[...], grad_rhs[...]).reshape(NSTN, SLOTS * MARGINS, MEMBERS)
        for peer in s_peers:
            send(ans_out.at[k, peer[0]], ans_in.at[k, stn], an_s.at[k], an_r.at[k], peer)
        ans_in[k, stn] = ans_out[k, stn]
        own = own_grad[...]
        square = column_sum(own * own)
        for j in range(NSTN):
            pair_out[k, j, 0:1] = own[j:j + 1]
            pair_out[k, j, 1:2] = square
        for peer in s_peers:
            send(pair_out.at[k, peer[0]], pair_in.at[k, stn], pr_s.at[k], pr_r.at[k], peer)
        pair_in[k, stn] = pair_out[k, stn]

    for n in range(SLOTS):
        for o in range(MARGINS):
            put_coeffs(n, o * CENTRES, CENTRES, gath[listed[n][o]])
        tanh_phi = jnp.tanh(times_basis(basis, n))
        slope[n] = 0.5 * (1.0 - tanh_phi * tanh_phi)
        put_cells(n, 0.5 * (1.0 + tanh_phi))
    station(0)
    predicted, _ = sum_cells(0)
    own_res[...] = observed[...] - predicted
    gather_cells(0, own_res[...])
    gradient, _ = adjoint(0, False)
    own_grad[...] = gradient

    norm = None
    for k in range(1, ITERS + 1):
        answer(k - 1)
        drain(ans_in.at[k - 1, 0:NSTN - 1], an_r.at[k - 1])
        tiles = ans_in[k - 1].reshape(CENTRES // 2, 2, SLOTS * MARGINS, MEMBERS)
        for n, tile in enumerate(interleave(tiles[:, 0], tiles[:, 1])):
            put_coeffs(n, 0, MEMBERS, tile.reshape(MEMBERS, MEMBERS))
            put_cells(n, slope[n] * times_basis(basis_r, n))
        station(k)

        def group_norm():
            drain(pair_in.at[k - 1, 0:NSTN - 1], pr_r.at[k - 1])
            return sum(pair_in[k - 1, i, 1:2] for i in range(NSTN))

        image, new_norm = sum_cells(k, group_norm)
        direction = jnp.concatenate([pair_in[k - 1, i, 0:1] for i in range(NSTN)], axis=0)
        if k > 1:
            ratio = new_norm / norm
            image = image + ratio * own_image[...]
            direction = direction + ratio * own_dir[...]
        norm = new_norm
        own_image[...] = image
        own_dir[...] = direction
        if k < ITERS:
            gather_cells(k, image)
            change, curvature = adjoint(k, True)
            step = norm / curvature
            own_grad[...] = own_grad[...] - step * change
        else:
            row_core[0] = column_sum(image * image)
            send(row_core.at[0], row_core_in.at[0], rc_s.at[0], rc_r.at[0], core_peer)
            drain(row_core_in.at[0], rc_r.at[0])
            row_y[0] = row_core[0] + row_core_in[0]
            for peer in y_peers:
                send(row_y.at[0], row_y_in.at[0, y], ry_s.at[0], ry_r.at[0], peer)
            row_y_in[0, y] = row_y[0]
            drain(row_y_in.at[0, 0:NY - 1], ry_r.at[0])
            row_s[0] = sum(row_y_in[0, i] for i in range(NY))
            for peer in s_peers:
                send(row_s.at[0], row_s_in.at[0, stn], rs_s.at[0], rs_r.at[0], peer)
            row_s_in[0, stn] = row_s[0]
            drain(row_s_in.at[0, 0:NSTN - 1], rs_r.at[0])
            step = norm / sum(row_s_in[0, i] for i in range(NSTN))
        own_res[...] = own_res[...] - step * image
        own_upd[...] = step * direction if k == 1 else own_upd[...] + step * direction

    updated[...] = controls[...] + own_upd[...]
    final_residual[...] = own_res[...]

    drain(gath.at[0:NZ - 1], gz_s)
    drain(gath.at[0:NSTN - NZ], gx_s)
    drain(list_in.at[0:NSTN - 1], li_s)
    for k in range(ITERS + 1):
        drain(core_in.at[k], c_s.at[k])
        drain(y_in.at[k, 0:NY - 1], y_s.at[k])
        drain(row_core_in.at[k], rc_s.at[k])
        drain(row_y_in.at[k, 0:NY - 1], ry_s.at[k])
    for k in range(ITERS):
        drain(full.at[k, 0:NY - 1, 0], fy_s.at[k])
        drain(full.at[k, :, 0], fc_s.at[k])
        drain(scat_in.at[k, 0:NSTN - 1], sc_s.at[k])
        drain(ans_in.at[k, 0:NSTN - 1], an_s.at[k])
        drain(row_s_in.at[k, 0:NSTN - 1], rs_s.at[k])
        drain(pair_in.at[k, 0:NSTN - 1], pr_s.at[k])


def local(sensitivity, block_list, margin, centres, controls, observed):
    rows = (CENTRES, MEMBERS)
    a, d = ITERS + 1, ITERS

    def vmem(*shape):
        return pltpu.VMEM(shape, F32)

    entries = SLOTS * MARGINS
    scratch = [
        pltpu.VMEM((SLOTS, BLOCK, BLOCK), BF16),
        pltpu.VMEM((SLOTS, BLOCK, BLOCK), BF16),
        pltpu.VMEM((SLOTS, BLOCK, 2 * MEMBERS), BF16),
        pltpu.VMEM((SLOTS, BLOCK, 2 * MEMBERS), BF16),
        pltpu.VMEM((SLOTS, 2 * MEMBERS, BLOCK), BF16),
        pltpu.VMEM((SLOTS, 2 * MEMBERS, 2 * MEMBERS), BF16),
        pltpu.VMEM((SLOTS, BLOCK, 2 * MEMBERS), BF16),
        pltpu.VMEM((BLOCK, 2 * MEMBERS), BF16),
        vmem(SLOTS, BLOCK, MEMBERS),
        vmem(NSTN, entries, MEMBERS),
        pltpu.VMEM((NSTN * entries, MEMBERS), BF16),
        pltpu.VMEM((NSTN, NSTN * entries), BF16),
        pltpu.VMEM((MEMBERS, 2 * MEMBERS), BF16),
        pltpu.VMEM((NSTN * entries, 2 * MEMBERS), BF16),
        vmem(NSTN, *rows),
        vmem(a, NY, 2, *rows),
        vmem(a, NY, *rows),
        vmem(a, NY, *rows),
        vmem(a, NY, *rows),
        vmem(d, NY, 2, *rows),
        vmem(d, CENTRES // 2, 2, entries, MEMBERS),
        vmem(d, NSTN, entries, MEMBERS),
        vmem(d, NSTN, entries, MEMBERS),
        vmem(d, NSTN, entries, MEMBERS),
        vmem(*rows), vmem(*rows), vmem(*rows), vmem(*rows), vmem(*rows),
        vmem(a, 1, MEMBERS), vmem(a, 1, MEMBERS),
        vmem(a, 1, MEMBERS), vmem(a, NY, 1, MEMBERS),
        vmem(d, 1, MEMBERS), vmem(d, NSTN, 1, MEMBERS),
        vmem(d, NSTN, 2, MEMBERS), vmem(d, NSTN, 2, MEMBERS),
    ]
    scratch += [pltpu.SemaphoreType.DMA] * 7
    scratch += [pltpu.SemaphoreType.DMA((a,))] * 4
    scratch += [pltpu.SemaphoreType.DMA((d,))] * 8
    scratch += [pltpu.SemaphoreType.DMA((a,))] * 4
    scratch += [pltpu.SemaphoreType.DMA((d,))] * 4
    in_vmem = pl.BlockSpec(memory_space=pltpu.VMEM)
    in_smem = pl.BlockSpec(memory_space=pltpu.SMEM)
    return pl.pallas_call(
        kernel,
        out_shape=(jax.ShapeDtypeStruct(rows, F32), jax.ShapeDtypeStruct(rows, F32)),
        in_specs=[pl.BlockSpec(memory_space=pl.ANY), in_smem, in_smem, in_vmem, in_vmem, in_vmem],
        out_specs=(in_vmem, in_vmem),
        scratch_shapes=scratch,
        compiler_params=pltpu.CompilerParams(
            collective_id=0, has_side_effects=True, vmem_limit_bytes=40 * 1024 * 1024
        ),
        cost_estimate=pl.CostEstimate(flops=3_000_000_000, bytes_accessed=2_000_000, transcendentals=262144),
        name="gauss_newton",
    )(
        sensitivity.reshape(SLOTS, BLOCK, BLOCK), block_list.reshape(SLOTS), margin, centres,
        controls, observed,
    )


def solution(mesh):
    return jax.shard_map(
        local,
        mesh=mesh,
        in_specs=(
            P("stn", "cell", None, None, None),
            P("stn", "cell", None),
            P("cell", None),
            P("cell", None),
            P(("stn", "cell"), None),
            P(("stn", "cell"), None),
        ),
        out_specs=(P(("stn", "cell"), None), P(("stn", "cell"), None)),
        check_vma=False,
    )
```

time: 188 us -> 149 us (0.79)
  Pallas kernels: 182 us -> 145 us
    pallas_call x1, Pallas kernels: 182 us -> 145 us  [local(): pl.pallas_call(kernel, out_shape=(jax.ShapeDtypeStruct(rows, F32), jax.Sh...]
where the time goes in v2:
time: 149 us
  Pallas kernels  145 us (97%)
  local copies, waits for them, and re-layouts  3.24 us (2%)
    pallas_call x1, Pallas kernels, local(): pl.pallas_call(kernel, out_shape=(jax.ShapeDtypeStruct(rows, F32), jax.Sh...  145 us
    unnamed x13, local copies, waits for them, and re-layouts  3.24 us

profile of v2, /device:TPU:1, one launch (start us, length us, event | category | flops | bytes accessed | tf_op | source)
XLA Modules:
  0.0 148.6 jit_solution(7734472097459599666)
XLA Ops:
  0.6 0.0 copy-start.3
  0.6 0.0 copy-start.1
  0.7 0.0 copy-start.2
  0.7 0.0 copy-start.4
  0.7 0.8 copy.8.margin
  1.5 0.0 copy-done.3
  1.5 0.0 copy-done.1
  1.5 0.0 copy-done.2
  1.5 0.0 copy-done.4
  1.5 0.0 copy-start
  1.5 1.2 copy-done
  2.7 144.6 %gauss_newton.1 = (f32[32,128]{1,0:T(8,128)S(1)}, f32[32,128]{1,0:T(8,128)S(1)}) custom-call(bf16[2,512,512]{2,1,0:T(8,128)(2,1)S(1)} %bitcast.2, s32[2]{0:T(128)S(1)} %bitcast.3, s32[64,4]{1,0:T(8,128)S(1)} %copy.8.margin, s32[1,1024]{1,0:T(1,128)S(1)} %copy-done.3, f32[32,128]{1,0:T(8,128)S(1)} %copy-done.1, f32[32,128]{1,0:T(8,128)S(1)} %copy-done.2), custom_call_target="tpu_custom_call" | custom-call | flops 3000000000 | bytes 2000000 | tf_op jit(solution)/shard_map/gauss_newton/pallas_call | solution.py:367
  147.4 0.6 copy.11
  148.0 0.6 copy.12
Async XLA Ops:
  0.6 0.8 copy-start.3
  0.6 0.8 copy-start.1
  0.7 0.8 copy-start.2
  0.7 0.8 copy-start.4
  1.5 1.2 copy-start

commit v3 on v2

--- a/solution.py
+++ b/solution.py
@@ -33,21 +33,33 @@
 def kernel(
     sens_hbm, blocks, margin, centres, controls, observed, updated, final_residual,
     sens, sens_t, basis, basis_r, basis_t, coeff_rhs, cell_rhs, row_rhs, slope,
-    list_in, hot, hot_t, grad_rhs, entry_rhs,
+    list_in, hot, hot_t, same, entry_rhs,
     gath, part, core_in, paired, y_in, full, scat_out, scat_in, ans_out, ans_in,
     own_grad, own_dir, own_image, own_res, own_upd,
-    row_core, row_core_in, row_y, row_y_in, row_s, row_s_in, pair_out, pair_in,
-    sens_sem, li_s, li_r, gz_s, gz_r, gx_s, gx_r, c_s, c_r, y_s, y_r, fy_s, fy_r, fc_s, fc_r,
+    row_core, row_core_in, row_y, row_y_in, row_s, row_s_in, row_c, row_c_in, pair_out, pair_in,
+    sens_sem, li_s, li_r, gz_s, gz_r, gx_s, gx_r, hx_s, hx_r, hz_s, hz_r, cc_s, cc_r,
+    c_s, c_r, y_s, y_r, fy_s, fy_r, fc_s, fc_r,
     sc_s, sc_r, an_s, an_r, rc_s, rc_r, ry_s, ry_r, rs_s, rs_r, pr_s, pr_r,
 ):
     stn, cell = lax.axis_index("stn"), lax.axis_index("cell")
     x, z = stn // NZ, stn % NZ
     y, core = cell // 2, cell % 2
-    x_peers = [((x + d) % NX, ((x + d) % NX) * NZ + z, cell) for d in range(1, NX)]
-    z_peers = [((z + d) % NZ, x * NZ + (z + d) % NZ, cell) for d in range(1, NZ)]
-    y_peers = [((y + d) % NY, stn, ((y + d) % NY) * 2 + core) for d in range(1, NY)]
+    def ring(size, step):
+        return min(step, size - step)
+
+    far_y = sorted(range(1, NY), key=lambda d: -ring(NY, d))
+    far_z = sorted(range(1, NZ), key=lambda d: -ring(NZ, d))
+    far_x = sorted(range(1, NX), key=lambda d: -ring(NX, d))
+    far_s = sorted(
+        [(a, b) for a in range(NX) for b in range(NZ) if a or b],
+        key=lambda d: -ring(NX, d[0]) - ring(NZ, d[1]),
+    )
+    x_peers = [((x + d) % NX, ((x + d) % NX) * NZ + z, cell) for d in far_x]
+    z_peers = [((z + d) % NZ, x * NZ + (z + d) % NZ, cell) for d in far_z]
+    y_peers = [((y + d) % NY, stn, ((y + d) % NY) * 2 + core) for d in far_y]
+    y_others = [((y + d) % NY, stn, ((y + d) % NY) * 2 + 1 - core) for d in far_y]
     core_peer = (1 - core, stn, y * 2 + 1 - core)
-    s_peers = [((stn + d) % NSTN, (stn + d) % NSTN, cell) for d in range(1, NSTN)]
+    s_peers = [((x + a) % NX * NZ + (z + b) % NZ, (x + a) % NX * NZ + (z + b) % NZ, cell) for a, b in far_s]
 
     def send(src, dst, ssem, rsem, peer):
         pltpu.make_async_remote_copy(
@@ -59,28 +71,33 @@
         pltpu.make_async_copy(ref, ref, sem).wait()
 
     barrier = pltpu.get_barrier_semaphore()
-    everyone = s_peers + y_peers + [core_peer]
+    everyone = s_peers + y_peers + y_others + [core_peer]
     for peer in everyone:
         pl.semaphore_signal(
             barrier, inc=1, device_id={"stn": peer[1], "cell": peer[2]}, device_id_type=MESH
         )
-    load = pltpu.make_async_copy(sens_hbm, sens, sens_sem)
-    load.start()
-    gath[stn] = controls[...]
+    loads = [
+        pltpu.make_async_copy(sens_hbm.at[n, :, side], sens.at[half, n], sens_sem.at[half * SLOTS + n])
+        for half, side in ((0, 1 - core), (1, core)) for n in range(SLOTS)
+    ]
+    for load in loads:
+        load.start()
+    gath[x, z] = controls[...]
     pl.semaphore_wait(barrier, len(everyone))
 
-    listed = [[margin[blocks[n], o] for o in range(MARGINS)] for n in range(SLOTS)]
+    most, rest = pl.ds(0, 24), pl.ds(24, 8)
+    for peer in z_peers:
+        send(gath.at[x, z, most], gath.at[x, z, most], gz_s, gz_r, peer)
+    for peer in x_peers:
+        send(gath.at[x, z, rest], gath.at[x, z, rest], hx_s, hx_r, peer)
+
+    listed = [[margin[o, blocks[n]] for o in range(MARGINS)] for n in range(SLOTS)]
     entry = lax.broadcasted_iota(jnp.int32, (SLOTS * MARGINS, MEMBERS), 0)
     lists = jnp.zeros((SLOTS * MARGINS, MEMBERS), F32)
     for n in range(SLOTS):
         for o in range(MARGINS):
             lists = jnp.where(entry == n * MARGINS + o, listed[n][o].astype(F32), lists)
     list_in[stn] = lists
-
-    for peer in z_peers:
-        send(gath.at[stn], gath.at[stn], gz_s, gz_r, peer)
-    for peer in s_peers:
-        send(list_in.at[stn], list_in.at[stn], li_s, li_r, peer)
 
     lane = lax.broadcasted_iota(jnp.int32, (8, MEMBERS), 1)
     rows_of_centres = [
@@ -120,22 +137,34 @@
         basis_t[n, 0:MEMBERS] = high.T.astype(BF16)
         basis_t[n, MEMBERS:] = low.T.astype(BF16)
 
-    drain(gath.at[0:NZ - 1], gz_r)
-    x_rows = pl.ds(x * NZ, NZ)
+    drain(gath.at[0, 0:NZ - 1, most], gz_r)
     for peer in x_peers:
-        send(gath.at[x_rows], gath.at[x_rows], gx_s, gx_r, peer)
-    load.wait()
-    for n in range(SLOTS):
-        for i in range(4):
-            piece = sens[n, i * 128:(i + 1) * 128, :]
-            sens_t[n, :, i * 128:(i + 1) * 128] = piece.T
-    drain(list_in.at[0:NSTN - 1], li_r)
-    flat_lists = list_in[...].reshape(NSTN * SLOTS * MARGINS, MEMBERS)
-    found = (flat_lists == lax.broadcasted_iota(jnp.int32, flat_lists.shape, 1).astype(F32)).astype(F32)
-    hot[...] = found.astype(BF16)
-    hot_t[...] = found.T[0:NSTN].astype(BF16)
-    grad_rhs[...] = jnp.zeros_like(grad_rhs)
-    drain(gath.at[0:NSTN - NZ], gx_r)
+        send(gath.at[x, :, most], gath.at[x, :, most], gx_s, gx_r, peer)
+    drain(gath.at[0:NX - 1, 0, rest], hx_r)
+    for peer in z_peers:
+        send(gath.at[:, z, rest], gath.at[:, z, rest], hz_s, hz_r, peer)
+    for load in loads:
+        load.wait()
+    for half in range(2):
+        for n in range(SLOTS):
+            for i in range(2):
+                piece = sens[half, n, i * 4:(i + 1) * 4].reshape(128, BLOCK)
+                sens_t[half, n, :, i * 128:(i + 1) * 128] = piece.T
+    drain(gath.at[0:NX - 1, :, most], gx_r)
+    drain(gath.at[:, 0:NZ - 1, rest], hz_r)
+
+    def send_lists():
+        for peer in s_peers:
+            send(list_in.at[stn], list_in.at[stn], li_s, li_r, peer)
+
+    def use_lists():
+        drain(list_in.at[0:NSTN - 1], li_r)
+        flat_lists = list_in[...].reshape(NSTN * SLOTS * MARGINS, MEMBERS)
+        found = (flat_lists == lax.broadcasted_iota(jnp.int32, flat_lists.shape, 1).astype(F32)).astype(F32)
+        hot[...] = found.astype(BF16)
+        found_t = found.T.astype(BF16)
+        hot_t[...] = found_t[0:NSTN]
+        same[...] = jnp.dot(hot[...], found_t, preferred_element_type=F32).astype(BF16)
 
     def times_basis(table, n):
         both = jnp.dot(table[n], coeff_rhs[n], preferred_element_type=F32)
@@ -151,26 +180,30 @@
         both = jnp.dot(left, rhs, preferred_element_type=F32)
         return both[:, 0:MEMBERS] + both[:, MEMBERS:]
 
-    def station(k):
-        both = jnp.dot(sens[0], cell_rhs[0], preferred_element_type=F32)
-        both += jnp.dot(sens[1], cell_rhs[1], preferred_element_type=F32)
-        part[k] = (both[:, 0:MEMBERS] + both[:, MEMBERS:]).reshape(NCELL // 2, 2, CENTRES, MEMBERS)
+    def station_rows(half):
+        both = jnp.dot(sens[half, 0].reshape(BLOCK // 2, BLOCK), cell_rhs[0], preferred_element_type=F32)
+        both += jnp.dot(sens[half, 1].reshape(BLOCK // 2, BLOCK), cell_rhs[1], preferred_element_type=F32)
+        return (both[:, 0:MEMBERS] + both[:, MEMBERS:]).reshape(NY, CENTRES, MEMBERS)
 
     def put_cells(n, value):
         high, low = split(value)
         cell_rhs[n, :, 0:MEMBERS] = high
         cell_rhs[n, :, MEMBERS:] = low
 
-    def sum_cells(k, group_norm=None):
-        send(part.at[k, :, 1 - core], core_in.at[k], c_s.at[k], c_r.at[k], core_peer)
+    def sum_cells(k, group_norm=None, meanwhile=None):
+        part[k] = station_rows(0)
+        send(part.at[k], core_in.at[k], c_s.at[k], c_r.at[k], core_peer)
+        own_rows = station_rows(1)
         if group_norm is not None:
             row_core[k] = group_norm()
             send(row_core.at[k], row_core_in.at[k], rc_s.at[k], rc_r.at[k], core_peer)
         drain(core_in.at[k], c_r.at[k])
-        paired[k] = part[k, :, core] + core_in[k]
+        paired[k] = own_rows + core_in[k]
         for peer in y_peers:
             send(paired.at[k, peer[0]], y_in.at[k, y], y_s.at[k], y_r.at[k], peer)
         y_in[k, y] = paired[k, y]
+        if meanwhile is not None:
+            meanwhile()
         norm = None
         if group_norm is not None:
             drain(row_core_in.at[k], rc_r.at[k])
@@ -184,26 +217,36 @@
         return sum(y_in[k, i] for i in range(NY)), norm
 
     def gather_cells(k, rows):
-        full[k, y, core] = rows
+        full[k, 1, y] = rows
         for peer in y_peers:
-            send(full.at[k, y, core], full.at[k, y, core], fy_s.at[k], fy_r.at[k], peer)
-        drain(full.at[k, 0:NY - 1, 0], fy_r.at[k])
-        send(full.at[k, :, core], full.at[k, :, core], fc_s.at[k], fc_r.at[k], core_peer)
-        drain(full.at[k, :, 0], fc_r.at[k])
+            send(full.at[k, 1, y], full.at[k, 1, y], fy_s.at[k], fy_r.at[k], peer)
+
+    def pull(k, half, n):
+        return both_ways(sens_t[half, n], row_rhs[half])
+
+    def put_rows(half, value):
+        high, low = split(value)
+        row_rhs[half, :, 0:MEMBERS] = high
+        row_rhs[half, :, MEMBERS:] = low
 
     def adjoint(k, with_curvature):
-        rows = full[k].reshape(BLOCK, MEMBERS)
+        drain(full.at[k, 1, 0:NY - 1], fy_r.at[k])
+        send(full.at[k, 1], full.at[k, 0], fc_s.at[k], fc_r.at[k], core_peer)
+        own_rows = full[k, 1].reshape(BLOCK // 2, MEMBERS)
+        put_rows(1, own_rows)
+        pulled = [pull(k, 1, n) for n in range(SLOTS)]
+        squares = column_sum(own_rows * own_rows)
+        drain(full.at[k, 0], fc_r.at[k])
+        rows = full[k, 0].reshape(BLOCK // 2, MEMBERS)
         if with_curvature:
-            row_s[k] = column_sum(rows * rows)
+            row_s[k] = squares + column_sum(rows * rows)
             for peer in s_peers:
                 send(row_s.at[k], row_s_in.at[k, stn], rs_s.at[k], rs_r.at[k], peer)
             row_s_in[k, stn] = row_s[k]
-        high, low = split(rows)
-        row_rhs[:, 0:MEMBERS] = high
-        row_rhs[:, MEMBERS:] = low
+        put_rows(0, rows)
         parts = []
         for n in range(SLOTS):
-            put_cells(n, slope[n] * both_ways(sens_t[n], row_rhs[...]))
+            put_cells(n, slope[n] * (pulled[n] + pull(k, 0, n)))
             two = both_ways(basis_t[n], cell_rhs[n])
             parts.append((two[0:MEMBERS] + two[MEMBERS:]).reshape(CENTRES // 2, 2 * MARGINS, MEMBERS))
         even, odd = interleave(parts[0], parts[1])
@@ -220,17 +263,19 @@
         high, low = split(scat_in[k].reshape(NSTN * SLOTS * MARGINS, MEMBERS))
         entry_rhs[:, 0:MEMBERS] = high
         entry_rhs[:, MEMBERS:] = low
-        return both_ways(hot_t[...], entry_rhs[...]), curvature
-
-    def answer(k):
-        high, low = split(own_grad[...])
-        grad_rhs[0:NSTN, 0:MEMBERS] = high
-        grad_rhs[0:NSTN, MEMBERS:] = low
-        ans_out[k] = both_ways(hot[...], grad_rhs[...]).reshape(NSTN, SLOTS * MARGINS, MEMBERS)
+        return curvature
+
+    def own_change():
+        return both_ways(hot_t[...], entry_rhs[...])
+
+    def answer(k, step=None):
+        change = both_ways(same[...], entry_rhs[...]).reshape(NSTN, SLOTS * MARGINS, MEMBERS)
+        ans_out[k] = change if step is None else ans_out[k - 1] - step * change
         for peer in s_peers:
             send(ans_out.at[k, peer[0]], ans_in.at[k, stn], an_s.at[k], an_r.at[k], peer)
         ans_in[k, stn] = ans_out[k, stn]
-        own = own_grad[...]
+        own = own_change() if step is None else own_grad[...] - step * own_change()
+        own_grad[...] = own
         square = column_sum(own * own)
         for j in range(NSTN):
             pair_out[k, j, 0:1] = own[j:j + 1]
@@ -241,26 +286,24 @@
 
     for n in range(SLOTS):
         for o in range(MARGINS):
-            put_coeffs(n, o * CENTRES, CENTRES, gath[listed[n][o]])
+            put_coeffs(n, o * CENTRES, CENTRES, gath[listed[n][o] // NZ, listed[n][o] % NZ])
         tanh_phi = jnp.tanh(times_basis(basis, n))
         slope[n] = 0.5 * (1.0 - tanh_phi * tanh_phi)
         put_cells(n, 0.5 * (1.0 + tanh_phi))
-    station(0)
-    predicted, _ = sum_cells(0)
+    predicted, _ = sum_cells(0, meanwhile=send_lists)
     own_res[...] = observed[...] - predicted
     gather_cells(0, own_res[...])
-    gradient, _ = adjoint(0, False)
-    own_grad[...] = gradient
+    use_lists()
+    adjoint(0, False)
+    answer(0)
 
     norm = None
     for k in range(1, ITERS + 1):
-        answer(k - 1)
         drain(ans_in.at[k - 1, 0:NSTN - 1], an_r.at[k - 1])
         tiles = ans_in[k - 1].reshape(CENTRES // 2, 2, SLOTS * MARGINS, MEMBERS)
         for n, tile in enumerate(interleave(tiles[:, 0], tiles[:, 1])):
             put_coeffs(n, 0, MEMBERS, tile.reshape(MEMBERS, MEMBERS))
             put_cells(n, slope[n] * times_basis(basis_r, n))
-        station(k)
 
         def group_norm():
             drain(pair_in.at[k - 1, 0:NSTN - 1], pr_r.at[k - 1])
@@ -277,19 +320,16 @@
         own_dir[...] = direction
         if k < ITERS:
             gather_cells(k, image)
-            change, curvature = adjoint(k, True)
+            curvature = adjoint(k, True)
             step = norm / curvature
-            own_grad[...] = own_grad[...] - step * change
+            answer(k, step)
         else:
-            row_core[0] = column_sum(image * image)
-            send(row_core.at[0], row_core_in.at[0], rc_s.at[0], rc_r.at[0], core_peer)
-            drain(row_core_in.at[0], rc_r.at[0])
-            row_y[0] = row_core[0] + row_core_in[0]
-            for peer in y_peers:
-                send(row_y.at[0], row_y_in.at[0, y], ry_s.at[0], ry_r.at[0], peer)
-            row_y_in[0, y] = row_y[0]
-            drain(row_y_in.at[0, 0:NY - 1], ry_r.at[0])
-            row_s[0] = sum(row_y_in[0, i] for i in range(NY))
+            row_c[...] = column_sum(image * image)
+            for peer in y_others + y_peers + [core_peer]:
+                send(row_c, row_c_in.at[cell], cc_s, cc_r, peer)
+            row_c_in[cell] = row_c[...]
+            drain(row_c_in.at[0:NCELL - 1], cc_r)
+            row_s[0] = sum(row_c_in[i] for i in range(NCELL))
             for peer in s_peers:
                 send(row_s.at[0], row_s_in.at[0, stn], rs_s.at[0], rs_r.at[0], peer)
             row_s_in[0, stn] = row_s[0]
@@ -301,17 +341,21 @@
     updated[...] = controls[...] + own_upd[...]
     final_residual[...] = own_res[...]
 
-    drain(gath.at[0:NZ - 1], gz_s)
-    drain(gath.at[0:NSTN - NZ], gx_s)
+    drain(gath.at[0, 0:NZ - 1, most], gz_s)
+    drain(gath.at[0:NX - 1, :, most], gx_s)
+    drain(gath.at[0:NX - 1, 0, rest], hx_s)
+    drain(gath.at[:, 0:NZ - 1, rest], hz_s)
+    drain(row_c_in.at[0:NCELL - 1], cc_s)
     drain(list_in.at[0:NSTN - 1], li_s)
     for k in range(ITERS + 1):
         drain(core_in.at[k], c_s.at[k])
         drain(y_in.at[k, 0:NY - 1], y_s.at[k])
+    for k in range(1, ITERS + 1):
         drain(row_core_in.at[k], rc_s.at[k])
         drain(row_y_in.at[k, 0:NY - 1], ry_s.at[k])
     for k in range(ITERS):
-        drain(full.at[k, 0:NY - 1, 0], fy_s.at[k])
-        drain(full.at[k, :, 0], fc_s.at[k])
+        drain(full.at[k, 1, 0:NY - 1], fy_s.at[k])
+        drain(full.at[k, 1], fc_s.at[k])
         drain(scat_in.at[k, 0:NSTN - 1], sc_s.at[k])
         drain(ans_in.at[k, 0:NSTN - 1], an_s.at[k])
         drain(row_s_in.at[k, 0:NSTN - 1], rs_s.at[k])
@@ -327,26 +371,26 @@
 
     entries = SLOTS * MARGINS
     scratch = [
-        pltpu.VMEM((SLOTS, BLOCK, BLOCK), BF16),
-        pltpu.VMEM((SLOTS, BLOCK, BLOCK), BF16),
+        pltpu.VMEM((2, SLOTS, NY, CENTRES, BLOCK), BF16),
+        pltpu.VMEM((2, SLOTS, BLOCK, BLOCK // 2), BF16),
         pltpu.VMEM((SLOTS, BLOCK, 2 * MEMBERS), BF16),
         pltpu.VMEM((SLOTS, BLOCK, 2 * MEMBERS), BF16),
         pltpu.VMEM((SLOTS, 2 * MEMBERS, BLOCK), BF16),
         pltpu.VMEM((SLOTS, 2 * MEMBERS, 2 * MEMBERS), BF16),
         pltpu.VMEM((SLOTS, BLOCK, 2 * MEMBERS), BF16),
-        pltpu.VMEM((BLOCK, 2 * MEMBERS), BF16),
+        pltpu.VMEM((2, BLOCK // 2, 2 * MEMBERS), BF16),
         vmem(SLOTS, BLOCK, MEMBERS),
         vmem(NSTN, entries, MEMBERS),
         pltpu.VMEM((NSTN * entries, MEMBERS), BF16),
         pltpu.VMEM((NSTN, NSTN * entries), BF16),
-        pltpu.VMEM((MEMBERS, 2 * MEMBERS), BF16),
+        pltpu.VMEM((NSTN * entries, NSTN * entries), BF16),
         pltpu.VMEM((NSTN * entries, 2 * MEMBERS), BF16),
-        vmem(NSTN, *rows),
-        vmem(a, NY, 2, *rows),
+        vmem(NX, NZ, *rows),
         vmem(a, NY, *rows),
         vmem(a, NY, *rows),
         vmem(a, NY, *rows),
-        vmem(d, NY, 2, *rows),
+        vmem(a, NY, *rows),
+        vmem(d, 2, NY, *rows),
         vmem(d, CENTRES // 2, 2, entries, MEMBERS),
         vmem(d, NSTN, entries, MEMBERS),
         vmem(d, NSTN, entries, MEMBERS),
@@ -355,9 +399,11 @@
         vmem(a, 1, MEMBERS), vmem(a, 1, MEMBERS),
         vmem(a, 1, MEMBERS), vmem(a, NY, 1, MEMBERS),
         vmem(d, 1, MEMBERS), vmem(d, NSTN, 1, MEMBERS),
+        vmem(1, MEMBERS), vmem(NCELL, 1, MEMBERS),
         vmem(d, NSTN, 2, MEMBERS), vmem(d, NSTN, 2, MEMBERS),
     ]
-    scratch += [pltpu.SemaphoreType.DMA] * 7
+    scratch += [pltpu.SemaphoreType.DMA((2 * SLOTS,))]
+    scratch += [pltpu.SemaphoreType.DMA] * 12
     scratch += [pltpu.SemaphoreType.DMA((a,))] * 4
     scratch += [pltpu.SemaphoreType.DMA((d,))] * 8
     scratch += [pltpu.SemaphoreType.DMA((a,))] * 4
@@ -371,12 +417,12 @@
         out_specs=(in_vmem, in_vmem),
         scratch_shapes=scratch,
         compiler_params=pltpu.CompilerParams(
-            collective_id=0, has_side_effects=True, vmem_limit_bytes=40 * 1024 * 1024
+            collective_id=0, has_side_effects=True, vmem_limit_bytes=60 * 1024 * 1024
         ),
         cost_estimate=pl.CostEstimate(flops=3_000_000_000, bytes_accessed=2_000_000, transcendentals=262144),
         name="gauss_newton",
     )(
-        sensitivity.reshape(SLOTS, BLOCK, BLOCK), block_list.reshape(SLOTS), margin, centres,
+        sensitivity.reshape(SLOTS, NY, 2, CENTRES, BLOCK), block_list.reshape(SLOTS), margin.T, centres,
         controls, observed,
     )
 

time: 149 us -> 136 us (0.913)
  Pallas kernels: 145 us -> 133 us
    pallas_call x1, Pallas kernels: 145 us -> 133 us  [local(): pl.pallas_call(kernel, out_shape=(jax.ShapeDtypeStruct(rows, F32), jax.Sh...]
    unnamed x13 -> x4, local copies, waits for them, and re-layouts: 3.24 us -> 1.94 us
where the time goes in v3:
time: 136 us; the launch traced here: 135 us
  Pallas kernels  133 us (98%)
  local copies, waits for them, and re-layouts  1.94 us (1%)
    pallas_call x1, Pallas kernels, local(): pl.pallas_call(kernel, out_shape=(jax.ShapeDtypeStruct(rows, F32), jax.Sh...  133 us

profile of v3, /device:TPU:1, one launch (start us, length us, event | category | flops | bytes accessed | tf_op | source)
XLA Modules:
  0.0 135.5 jit_solution(7732782682411199758)
XLA Ops:
  0.6 132.9 %gauss_newton.1 = (f32[32,128]{1,0:T(8,128)}, f32[32,128]{1,0:T(8,128)}) custom-call(bf16[2,8,2,32,512]{4,3,2,1,0:T(8,128)(2,1)} %bitcast.3, s32[2]{0:T(128)} %bitcast.5, s32[4,64]{1,0:T(4,128)} %bitcast.4, s32[1,1024]{1,0:T(1,128)} %centres.1, f32[32,128]{1,0:T(8,128)} %controls.1, f32[32,128]{1,0:T(8,128)} %observed.1), custom_call_target="tpu_custom_call" | custom-call | flops 3000000000 | bytes 2000000 | tf_op jit(solution)/shard_map/gauss_newton/pallas_call | solution.py:413
  133.5 0.0 copy-start
  133.5 1.3 copy.10
  134.9 0.0 copy-done
  134.9 0.6 copy.11
Async XLA Ops:
  133.5 1.3 copy-start

commit v4 on v3

--- a/solution.py
+++ b/solution.py
@@ -31,8 +31,8 @@
 
 
 def kernel(
-    sens_hbm, blocks, margin, centres, controls, observed, updated, final_residual,
-    sens, sens_t, basis, basis_r, basis_t, coeff_rhs, cell_rhs, row_rhs, slope,
+    sens_hbm, blocks, margin, centres, controls, observed, outputs,
+    sens, sens_t, basis, basis_r, basis_t, coeff_rhs, cell_rhs, row_rhs, slope, pulled,
     list_in, hot, hot_t, same, entry_rhs,
     gath, part, core_in, paired, y_in, full, scat_out, scat_in, ans_out, ans_in,
     own_grad, own_dir, own_image, own_res, own_upd,
@@ -71,7 +71,7 @@
         pltpu.make_async_copy(ref, ref, sem).wait()
 
     barrier = pltpu.get_barrier_semaphore()
-    everyone = s_peers + y_peers + y_others + [core_peer]
+    everyone = z_peers + y_peers + x_peers + [core_peer]
     for peer in everyone:
         pl.semaphore_signal(
             barrier, inc=1, device_id={"stn": peer[1], "cell": peer[2]}, device_id_type=MESH
@@ -149,7 +149,7 @@
         for n in range(SLOTS):
             for i in range(2):
                 piece = sens[half, n, i * 4:(i + 1) * 4].reshape(128, BLOCK)
-                sens_t[half, n, :, i * 128:(i + 1) * 128] = piece.T
+                sens_t[half, n * BLOCK:(n + 1) * BLOCK, i * 128:(i + 1) * 128] = piece.T
     drain(gath.at[0:NX - 1, :, most], gx_r)
     drain(gath.at[:, 0:NZ - 1, rest], hz_r)
 
@@ -189,6 +189,17 @@
         high, low = split(value)
         cell_rhs[n, :, 0:MEMBERS] = high
         cell_rhs[n, :, MEMBERS:] = low
+
+    def share_row(i):
+        drain(row_core_in.at[i], rc_r.at[i])
+        row_y[i] = row_core[i] + row_core_in[i]
+        for peer in y_peers:
+            send(row_y.at[i], row_y_in.at[i, y], ry_s.at[i], ry_r.at[i], peer)
+        row_y_in[i, y] = row_y[i]
+
+    def shared_row(i):
+        drain(row_y_in.at[i, 0:NY - 1], ry_r.at[i])
+        return sum(row_y_in[i, j] for j in range(NY))
 
     def sum_cells(k, group_norm=None, meanwhile=None):
         part[k] = station_rows(0)
@@ -206,23 +217,23 @@
             meanwhile()
         norm = None
         if group_norm is not None:
-            drain(row_core_in.at[k], rc_r.at[k])
-            row_y[k] = row_core[k] + row_core_in[k]
-            for peer in y_peers:
-                send(row_y.at[k], row_y_in.at[k, y], ry_s.at[k], ry_r.at[k], peer)
-            row_y_in[k, y] = row_y[k]
-            drain(row_y_in.at[k, 0:NY - 1], ry_r.at[k])
-            norm = sum(row_y_in[k, i] for i in range(NY))
+            share_row(k)
+            norm = shared_row(k)
         drain(y_in.at[k, 0:NY - 1], y_r.at[k])
         return sum(y_in[k, i] for i in range(NY)), norm
 
-    def gather_cells(k, rows):
+    def gather_cells(k, rows, with_curvature=True):
         full[k, 1, y] = rows
         for peer in y_peers:
             send(full.at[k, 1, y], full.at[k, 1, y], fy_s.at[k], fy_r.at[k], peer)
-
-    def pull(k, half, n):
-        return both_ways(sens_t[half, n], row_rhs[half])
+        if with_curvature:
+            row_s[k] = column_sum(rows * rows)
+            for peer in s_peers:
+                send(row_s.at[k], row_s_in.at[k, stn], rs_s.at[k], rs_r.at[k], peer)
+            row_s_in[k, stn] = row_s[k]
+
+    def pull(half):
+        return both_ways(sens_t[half], row_rhs[half]).reshape(SLOTS, BLOCK, MEMBERS)
 
     def put_rows(half, value):
         high, low = split(value)
@@ -232,21 +243,21 @@
     def adjoint(k, with_curvature):
         drain(full.at[k, 1, 0:NY - 1], fy_r.at[k])
         send(full.at[k, 1], full.at[k, 0], fc_s.at[k], fc_r.at[k], core_peer)
-        own_rows = full[k, 1].reshape(BLOCK // 2, MEMBERS)
-        put_rows(1, own_rows)
-        pulled = [pull(k, 1, n) for n in range(SLOTS)]
-        squares = column_sum(own_rows * own_rows)
+        put_rows(1, full[k, 1].reshape(BLOCK // 2, MEMBERS))
+        pulled[...] = pull(1)
+        if with_curvature:
+            drain(row_s_in.at[k, 0:NSTN - 1], rs_r.at[k])
+            row_core[ITERS + k] = sum(row_s_in[k, i] for i in range(NSTN))
+            send(row_core.at[ITERS + k], row_core_in.at[ITERS + k], rc_s.at[ITERS + k], rc_r.at[ITERS + k], core_peer)
         drain(full.at[k, 0], fc_r.at[k])
-        rows = full[k, 0].reshape(BLOCK // 2, MEMBERS)
+        put_rows(0, full[k, 0].reshape(BLOCK // 2, MEMBERS))
+        rest_of = pull(0)
+        for n in range(SLOTS):
+            put_cells(n, slope[n] * (pulled[n] + rest_of[n]))
         if with_curvature:
-            row_s[k] = squares + column_sum(rows * rows)
-            for peer in s_peers:
-                send(row_s.at[k], row_s_in.at[k, stn], rs_s.at[k], rs_r.at[k], peer)
-            row_s_in[k, stn] = row_s[k]
-        put_rows(0, rows)
+            share_row(ITERS + k)
         parts = []
         for n in range(SLOTS):
-            put_cells(n, slope[n] * (pulled[n] + pull(k, 0, n)))
             two = both_ways(basis_t[n], cell_rhs[n])
             parts.append((two[0:MEMBERS] + two[MEMBERS:]).reshape(CENTRES // 2, 2 * MARGINS, MEMBERS))
         even, odd = interleave(parts[0], parts[1])
@@ -257,8 +268,7 @@
         scat_in[k, stn] = scat_out[k, stn // 2, stn % 2]
         curvature = None
         if with_curvature:
-            drain(row_s_in.at[k, 0:NSTN - 1], rs_r.at[k])
-            curvature = sum(row_s_in[k, i] for i in range(NSTN))
+            curvature = shared_row(ITERS + k)
         drain(scat_in.at[k, 0:NSTN - 1], sc_r.at[k])
         high, low = split(scat_in[k].reshape(NSTN * SLOTS * MARGINS, MEMBERS))
         entry_rhs[:, 0:MEMBERS] = high
@@ -292,7 +302,7 @@
         put_cells(n, 0.5 * (1.0 + tanh_phi))
     predicted, _ = sum_cells(0, meanwhile=send_lists)
     own_res[...] = observed[...] - predicted
-    gather_cells(0, own_res[...])
+    gather_cells(0, own_res[...], False)
     use_lists()
     adjoint(0, False)
     answer(0)
@@ -303,30 +313,35 @@
         tiles = ans_in[k - 1].reshape(CENTRES // 2, 2, SLOTS * MARGINS, MEMBERS)
         for n, tile in enumerate(interleave(tiles[:, 0], tiles[:, 1])):
             put_coeffs(n, 0, MEMBERS, tile.reshape(MEMBERS, MEMBERS))
-            put_cells(n, slope[n] * times_basis(basis_r, n))
+        fields = [times_basis(basis_r, n) for n in range(SLOTS)]
+        for n in range(SLOTS):
+            put_cells(n, slope[n] * fields[n])
 
         def group_norm():
             drain(pair_in.at[k - 1, 0:NSTN - 1], pr_r.at[k - 1])
             return sum(pair_in[k - 1, i, 1:2] for i in range(NSTN))
 
         image, new_norm = sum_cells(k, group_norm)
+        ratio = new_norm / norm if k > 1 else None
+        if k > 1:
+            image = image + ratio * own_image[...]
+        norm = new_norm
+        own_image[...] = image
+        if k < ITERS:
+            gather_cells(k, image)
+        else:
+            row_c[...] = column_sum(image * image)
+            for peer in y_others + y_peers + [core_peer]:
+                send(row_c, row_c_in.at[cell], cc_s, cc_r, peer)
         direction = jnp.concatenate([pair_in[k - 1, i, 0:1] for i in range(NSTN)], axis=0)
         if k > 1:
-            ratio = new_norm / norm
-            image = image + ratio * own_image[...]
             direction = direction + ratio * own_dir[...]
-        norm = new_norm
-        own_image[...] = image
         own_dir[...] = direction
         if k < ITERS:
-            gather_cells(k, image)
             curvature = adjoint(k, True)
             step = norm / curvature
             answer(k, step)
         else:
-            row_c[...] = column_sum(image * image)
-            for peer in y_others + y_peers + [core_peer]:
-                send(row_c, row_c_in.at[cell], cc_s, cc_r, peer)
             row_c_in[cell] = row_c[...]
             drain(row_c_in.at[0:NCELL - 1], cc_r)
             row_s[0] = sum(row_c_in[i] for i in range(NCELL))
@@ -338,8 +353,8 @@
         own_res[...] = own_res[...] - step * image
         own_upd[...] = step * direction if k == 1 else own_upd[...] + step * direction
 
-    updated[...] = controls[...] + own_upd[...]
-    final_residual[...] = own_res[...]
+    outputs[0:CENTRES] = controls[...] + own_upd[...]
+    outputs[CENTRES:] = own_res[...]
 
     drain(gath.at[0, 0:NZ - 1, most], gz_s)
     drain(gath.at[0:NX - 1, :, most], gx_s)
@@ -350,7 +365,7 @@
     for k in range(ITERS + 1):
         drain(core_in.at[k], c_s.at[k])
         drain(y_in.at[k, 0:NY - 1], y_s.at[k])
-    for k in range(1, ITERS + 1):
+    for k in range(1, 2 * ITERS):
         drain(row_core_in.at[k], rc_s.at[k])
         drain(row_y_in.at[k, 0:NY - 1], ry_s.at[k])
     for k in range(ITERS):
@@ -364,7 +379,7 @@
 
 def local(sensitivity, block_list, margin, centres, controls, observed):
     rows = (CENTRES, MEMBERS)
-    a, d = ITERS + 1, ITERS
+    a, d, r = ITERS + 1, ITERS, 2 * ITERS
 
     def vmem(*shape):
         return pltpu.VMEM(shape, F32)
@@ -372,13 +387,14 @@
     entries = SLOTS * MARGINS
     scratch = [
         pltpu.VMEM((2, SLOTS, NY, CENTRES, BLOCK), BF16),
-        pltpu.VMEM((2, SLOTS, BLOCK, BLOCK // 2), BF16),
+        pltpu.VMEM((2, SLOTS * BLOCK, BLOCK // 2), BF16),
         pltpu.VMEM((SLOTS, BLOCK, 2 * MEMBERS), BF16),
         pltpu.VMEM((SLOTS, BLOCK, 2 * MEMBERS), BF16),
         pltpu.VMEM((SLOTS, 2 * MEMBERS, BLOCK), BF16),
         pltpu.VMEM((SLOTS, 2 * MEMBERS, 2 * MEMBERS), BF16),
         pltpu.VMEM((SLOTS, BLOCK, 2 * MEMBERS), BF16),
         pltpu.VMEM((2, BLOCK // 2, 2 * MEMBERS), BF16),
+        vmem(SLOTS, BLOCK, MEMBERS),
         vmem(SLOTS, BLOCK, MEMBERS),
         vmem(NSTN, entries, MEMBERS),
         pltpu.VMEM((NSTN * entries, MEMBERS), BF16),
@@ -396,8 +412,8 @@
         vmem(d, NSTN, entries, MEMBERS),
         vmem(d, NSTN, entries, MEMBERS),
         vmem(*rows), vmem(*rows), vmem(*rows), vmem(*rows), vmem(*rows),
-        vmem(a, 1, MEMBERS), vmem(a, 1, MEMBERS),
-        vmem(a, 1, MEMBERS), vmem(a, NY, 1, MEMBERS),
+        vmem(r, 1, MEMBERS), vmem(r, 1, MEMBERS),
+        vmem(r, 1, MEMBERS), vmem(r, NY, 1, MEMBERS),
         vmem(d, 1, MEMBERS), vmem(d, NSTN, 1, MEMBERS),
         vmem(1, MEMBERS), vmem(NCELL, 1, MEMBERS),
         vmem(d, NSTN, 2, MEMBERS), vmem(d, NSTN, 2, MEMBERS),
@@ -406,15 +422,15 @@
     scratch += [pltpu.SemaphoreType.DMA] * 12
     scratch += [pltpu.SemaphoreType.DMA((a,))] * 4
     scratch += [pltpu.SemaphoreType.DMA((d,))] * 8
-    scratch += [pltpu.SemaphoreType.DMA((a,))] * 4
+    scratch += [pltpu.SemaphoreType.DMA((r,))] * 4
     scratch += [pltpu.SemaphoreType.DMA((d,))] * 4
     in_vmem = pl.BlockSpec(memory_space=pltpu.VMEM)
     in_smem = pl.BlockSpec(memory_space=pltpu.SMEM)
-    return pl.pallas_call(
+    outputs = pl.pallas_call(
         kernel,
-        out_shape=(jax.ShapeDtypeStruct(rows, F32), jax.ShapeDtypeStruct(rows, F32)),
+        out_shape=jax.ShapeDtypeStruct((2 * CENTRES, MEMBERS), F32),
         in_specs=[pl.BlockSpec(memory_space=pl.ANY), in_smem, in_smem, in_vmem, in_vmem, in_vmem],
-        out_specs=(in_vmem, in_vmem),
+        out_specs=in_vmem,
         scratch_shapes=scratch,
         compiler_params=pltpu.CompilerParams(
             collective_id=0, has_side_effects=True, vmem_limit_bytes=60 * 1024 * 1024
@@ -425,6 +441,7 @@
         sensitivity.reshape(SLOTS, NY, 2, CENTRES, BLOCK), block_list.reshape(SLOTS), margin.T, centres,
         controls, observed,
     )
+    return outputs[:CENTRES], outputs[CENTRES:]
 
 
 def solution(mesh):

time: 136 us -> 134 us (0.985)
    unnamed x4 -> x0, local copies, waits for them, and re-layouts: 1.94 us -> none
where the time goes in v4:
time: 134 us
  Pallas kernels  132 us (99%)
  local copies, waits for them, and re-layouts  1.35 us (1%)
    pallas_call x1, Pallas kernels, local(): pl.pallas_call(kernel, out_shape=jax.ShapeDtypeStruct((2 * CENTRES, MEMBE...  132 us

profile of v4, /device:TPU:1, one launch (start us, length us, event | category | flops | bytes accessed | tf_op | source)
XLA Modules:
  0.0 133.7 jit_solution(9374974508744726359)
XLA Ops:
  0.6 131.7 %gauss_newton.1 = f32[64,128]{1,0:T(8,128)} custom-call(bf16[2,8,2,32,512]{4,3,2,1,0:T(8,128)(2,1)} %bitcast.3, s32[2]{0:T(128)} %bitcast.5, s32[4,64]{1,0:T(4,128)} %bitcast.4, s32[1,1024]{1,0:T(1,128)} %centres.1, f32[32,128]{1,0:T(8,128)} %controls.1, f32[32,128]{1,0:T(8,128)} %observed.1), custom_call_target="tpu_custom_call" | custom-call | flops 3000000000 | bytes 2000000 | tf_op jit(solution)/shard_map/gauss_newton/pallas_call | solution.py:429
  132.3 1.3 %fusion = (f32[32,128]{1,0:T(8,128)}, f32[32,128]{1,0:T(8,128)}) fusion(f32[64,128]{1,0:T(8,128)} %gauss_newton.1), kind=kLoop, calls=%fused_computation | loop fusion | bytes 65536 | tf_op jit(solution)/shard_map/slice | solution.py:444

commit v5 on v4

--- a/solution.py
+++ b/solution.py
@@ -31,13 +31,13 @@
 
 
 def kernel(
-    sens_hbm, blocks, margin, centres, controls, observed, outputs,
-    sens, sens_t, basis, basis_r, basis_t, coeff_rhs, cell_rhs, row_rhs, slope, pulled,
+    sens_hbm, blocks_hbm, margin_hbm, centres_hbm, controls, observed_hbm, outputs,
+    blocks, margin, centres, observed, sens, sens_t, basis, basis_r, basis_t, coeff_rhs, cell_rhs, row_rhs, slope, pulled,
     list_in, hot, hot_t, same, entry_rhs,
     gath, part, core_in, paired, y_in, full, scat_out, scat_in, ans_out, ans_in,
     own_grad, own_dir, own_image, own_res, own_upd,
     row_core, row_core_in, row_y, row_y_in, row_s, row_s_in, row_c, row_c_in, pair_out, pair_in,
-    sens_sem, li_s, li_r, gz_s, gz_r, gx_s, gx_r, hx_s, hx_r, hz_s, hz_r, cc_s, cc_r,
+    sens_sem, blocks_sem, margin_sem, centres_sem, controls_sem, observed_sem, li_s, li_r, gz_s, gz_r, gx_s, gx_r, hx_s, hx_r, hz_s, hz_r, cc_s, cc_r,
     c_s, c_r, y_s, y_r, fy_s, fy_r, fc_s, fc_r,
     sc_s, sc_r, an_s, an_r, rc_s, rc_r, ry_s, ry_r, rs_s, rs_r, pr_s, pr_r,
 ):
@@ -76,13 +76,23 @@
         pl.semaphore_signal(
             barrier, inc=1, device_id={"stn": peer[1], "cell": peer[2]}, device_id_type=MESH
         )
-    loads = [
-        pltpu.make_async_copy(sens_hbm.at[n, :, side], sens.at[half, n], sens_sem.at[half * SLOTS + n])
-        for half, side in ((0, 1 - core), (1, core)) for n in range(SLOTS)
+    first = pltpu.make_async_copy(controls, gath.at[x, z], controls_sem)
+    first.start()
+    small = [
+        pltpu.make_async_copy(src, dst, sem) for src, dst, sem in (
+            (blocks_hbm, blocks, blocks_sem), (margin_hbm, margin, margin_sem),
+            (centres_hbm, centres, centres_sem), (observed_hbm, observed, observed_sem),
+        )
     ]
-    for load in loads:
-        load.start()
-    gath[x, z] = controls[...]
+    for copy in small:
+        copy.start()
+    for half, side in ((0, 1 - core), (1, core)):
+        for n in range(SLOTS):
+            for p, d in enumerate(far_y + [0]):
+                pltpu.make_async_copy(
+                    sens_hbm.at[n, (y + d) % NY, side], sens.at[half, n, p], sens_sem.at[half * SLOTS + n]
+                ).start()
+    first.wait()
     pl.semaphore_wait(barrier, len(everyone))
 
     most, rest = pl.ds(0, 24), pl.ds(24, 8)
@@ -91,7 +101,9 @@
     for peer in x_peers:
         send(gath.at[x, z, rest], gath.at[x, z, rest], hx_s, hx_r, peer)
 
-    listed = [[margin[o, blocks[n]] for o in range(MARGINS)] for n in range(SLOTS)]
+    for copy in small:
+        copy.wait()
+    listed = [[margin[o, blocks[0, n]] for o in range(MARGINS)] for n in range(SLOTS)]
     entry = lax.broadcasted_iota(jnp.int32, (SLOTS * MARGINS, MEMBERS), 0)
     lists = jnp.zeros((SLOTS * MARGINS, MEMBERS), F32)
     for n in range(SLOTS):
@@ -107,7 +119,7 @@
     to_col = lax.broadcasted_iota(jnp.int32, (MEMBERS, MEMBERS), 1)
     by_row = (to_row == (to_col % MARGINS) * CENTRES + to_col // MARGINS).astype(BF16)
     for n in range(SLOTS):
-        block = blocks[n]
+        block = blocks[0, n]
         centre = jnp.zeros((8, MEMBERS), jnp.int32)
         for o in range(MARGINS):
             j = listed[n][o]
@@ -143,10 +155,9 @@
     drain(gath.at[0:NX - 1, 0, rest], hx_r)
     for peer in z_peers:
         send(gath.at[:, z, rest], gath.at[:, z, rest], hz_s, hz_r, peer)
-    for load in loads:
-        load.wait()
     for half in range(2):
         for n in range(SLOTS):
+            drain(sens.at[half, n], sens_sem.at[half * SLOTS + n])
             for i in range(2):
                 piece = sens[half, n, i * 4:(i + 1) * 4].reshape(128, BLOCK)
                 sens_t[half, n * BLOCK:(n + 1) * BLOCK, i * 128:(i + 1) * 128] = piece.T
@@ -201,18 +212,23 @@
         drain(row_y_in.at[i, 0:NY - 1], ry_r.at[i])
         return sum(row_y_in[i, j] for j in range(NY))
 
+    groups = (slice(0, 3), slice(3, NY))
+    place = {d: p for p, d in enumerate(far_y + [0])}
+
     def sum_cells(k, group_norm=None, meanwhile=None):
         part[k] = station_rows(0)
-        send(part.at[k], core_in.at[k], c_s.at[k], c_r.at[k], core_peer)
+        for g, blocks_of in enumerate(groups):
+            send(part.at[k, blocks_of], core_in.at[k, blocks_of], c_s.at[2 * k + g], c_r.at[2 * k + g], core_peer)
         own_rows = station_rows(1)
         if group_norm is not None:
             row_core[k] = group_norm()
             send(row_core.at[k], row_core_in.at[k], rc_s.at[k], rc_r.at[k], core_peer)
-        drain(core_in.at[k], c_r.at[k])
-        paired[k] = own_rows + core_in[k]
-        for peer in y_peers:
-            send(paired.at[k, peer[0]], y_in.at[k, y], y_s.at[k], y_r.at[k], peer)
-        y_in[k, y] = paired[k, y]
+        for g, blocks_of in enumerate(groups):
+            drain(core_in.at[k, blocks_of], c_r.at[2 * k + g])
+            paired[k, blocks_of] = own_rows[blocks_of] + core_in[k, blocks_of]
+            for p, peer in list(enumerate(y_peers))[blocks_of]:
+                send(paired.at[k, p], y_in.at[k, y], y_s.at[k], y_r.at[k], peer)
+        y_in[k, y] = paired[k, NY - 1]
         if meanwhile is not None:
             meanwhile()
         norm = None
@@ -223,9 +239,13 @@
         return sum(y_in[k, i] for i in range(NY)), norm
 
     def gather_cells(k, rows, with_curvature=True):
-        full[k, 1, y] = rows
-        for peer in y_peers:
-            send(full.at[k, 1, y], full.at[k, 1, y], fy_s.at[k], fy_r.at[k], peer)
+        full[k, 1, NY - 1] = rows
+        for p, peer in enumerate(y_peers):
+            g = int(p >= 3)
+            send(
+                full.at[k, 1, NY - 1], full.at[k, 1, place[NY - far_y[p]]],
+                fy_s.at[2 * k + g], fy_r.at[2 * k + g], peer,
+            )
         if with_curvature:
             row_s[k] = column_sum(rows * rows)
             for peer in s_peers:
@@ -241,15 +261,20 @@
         row_rhs[half, :, MEMBERS:] = low
 
     def adjoint(k, with_curvature):
-        drain(full.at[k, 1, 0:NY - 1], fy_r.at[k])
-        send(full.at[k, 1], full.at[k, 0], fc_s.at[k], fc_r.at[k], core_peer)
+        for g, arrived in ((1, slice(3, NY - 1)), (0, slice(0, 3))):
+            drain(full.at[k, 1, arrived], fy_r.at[2 * k + g])
+            send(
+                full.at[k, 1, groups[g]], full.at[k, 0, groups[g]],
+                fc_s.at[2 * k + g], fc_r.at[2 * k + g], core_peer,
+            )
         put_rows(1, full[k, 1].reshape(BLOCK // 2, MEMBERS))
         pulled[...] = pull(1)
         if with_curvature:
             drain(row_s_in.at[k, 0:NSTN - 1], rs_r.at[k])
             row_core[ITERS + k] = sum(row_s_in[k, i] for i in range(NSTN))
             send(row_core.at[ITERS + k], row_core_in.at[ITERS + k], rc_s.at[ITERS + k], rc_r.at[ITERS + k], core_peer)
-        drain(full.at[k, 0], fc_r.at[k])
+        for g in (1, 0):
+            drain(full.at[k, 0, groups[g]], fc_r.at[2 * k + g])
         put_rows(0, full[k, 0].reshape(BLOCK // 2, MEMBERS))
         rest_of = pull(0)
         for n in range(SLOTS):
@@ -353,7 +378,7 @@
         own_res[...] = own_res[...] - step * image
         own_upd[...] = step * direction if k == 1 else own_upd[...] + step * direction
 
-    outputs[0:CENTRES] = controls[...] + own_upd[...]
+    outputs[0:CENTRES] = gath[x, z] + own_upd[...]
     outputs[CENTRES:] = own_res[...]
 
     drain(gath.at[0, 0:NZ - 1, most], gz_s)
@@ -363,14 +388,16 @@
     drain(row_c_in.at[0:NCELL - 1], cc_s)
     drain(list_in.at[0:NSTN - 1], li_s)
     for k in range(ITERS + 1):
-        drain(core_in.at[k], c_s.at[k])
+        for g in range(2):
+            drain(core_in.at[k, groups[g]], c_s.at[2 * k + g])
         drain(y_in.at[k, 0:NY - 1], y_s.at[k])
     for k in range(1, 2 * ITERS):
         drain(row_core_in.at[k], rc_s.at[k])
         drain(row_y_in.at[k, 0:NY - 1], ry_s.at[k])
     for k in range(ITERS):
-        drain(full.at[k, 1, 0:NY - 1], fy_s.at[k])
-        drain(full.at[k, 1], fc_s.at[k])
+        for g, arrived in ((1, slice(3, NY - 1)), (0, slice(0, 3))):
+            drain(full.at[k, 1, arrived], fy_s.at[2 * k + g])
+            drain(full.at[k, 0, groups[g]], fc_s.at[2 * k + g])
         drain(scat_in.at[k, 0:NSTN - 1], sc_s.at[k])
         drain(ans_in.at[k, 0:NSTN - 1], an_s.at[k])
         drain(row_s_in.at[k, 0:NSTN - 1], rs_s.at[k])
@@ -386,6 +413,10 @@
 
     entries = SLOTS * MARGINS
     scratch = [
+        pltpu.SMEM((1, SLOTS), jnp.int32),
+        pltpu.SMEM((MARGINS, margin.shape[0]), jnp.int32),
+        pltpu.VMEM(centres.shape, jnp.int32),
+        vmem(*rows),
         pltpu.VMEM((2, SLOTS, NY, CENTRES, BLOCK), BF16),
         pltpu.VMEM((2, SLOTS * BLOCK, BLOCK // 2), BF16),
         pltpu.VMEM((SLOTS, BLOCK, 2 * MEMBERS), BF16),
@@ -419,17 +450,18 @@
         vmem(d, NSTN, 2, MEMBERS), vmem(d, NSTN, 2, MEMBERS),
     ]
     scratch += [pltpu.SemaphoreType.DMA((2 * SLOTS,))]
-    scratch += [pltpu.SemaphoreType.DMA] * 12
-    scratch += [pltpu.SemaphoreType.DMA((a,))] * 4
-    scratch += [pltpu.SemaphoreType.DMA((d,))] * 8
+    scratch += [pltpu.SemaphoreType.DMA] * 17
+    scratch += [pltpu.SemaphoreType.DMA((2 * a,))] * 2
+    scratch += [pltpu.SemaphoreType.DMA((a,))] * 2
+    scratch += [pltpu.SemaphoreType.DMA((2 * d,))] * 4
+    scratch += [pltpu.SemaphoreType.DMA((d,))] * 4
     scratch += [pltpu.SemaphoreType.DMA((r,))] * 4
     scratch += [pltpu.SemaphoreType.DMA((d,))] * 4
     in_vmem = pl.BlockSpec(memory_space=pltpu.VMEM)
-    in_smem = pl.BlockSpec(memory_space=pltpu.SMEM)
     outputs = pl.pallas_call(
         kernel,
         out_shape=jax.ShapeDtypeStruct((2 * CENTRES, MEMBERS), F32),
-        in_specs=[pl.BlockSpec(memory_space=pl.ANY), in_smem, in_smem, in_vmem, in_vmem, in_vmem],
+        in_specs=[pl.BlockSpec(memory_space=pl.ANY)] * 6,
         out_specs=in_vmem,
         scratch_shapes=scratch,
         compiler_params=pltpu.CompilerParams(
@@ -438,7 +470,7 @@
         cost_estimate=pl.CostEstimate(flops=3_000_000_000, bytes_accessed=2_000_000, transcendentals=262144),
         name="gauss_newton",
     )(
-        sensitivity.reshape(SLOTS, NY, 2, CENTRES, BLOCK), block_list.reshape(SLOTS), margin.T, centres,
+        sensitivity.reshape(SLOTS, NY, 2, CENTRES, BLOCK), block_list.reshape(1, SLOTS), margin.T, centres,
         controls, observed,
     )
     return outputs[:CENTRES], outputs[CENTRES:]

time: 134 us -> 134 us (level)
  no operation moved by 1% of the time
where the time goes in v5:
time: 134 us; the launch traced here: 133 us
  Pallas kernels  132 us (99%)
  local copies, waits for them, and re-layouts  1.35 us (1%)
    pallas_call x1, Pallas kernels, local(): pl.pallas_call(kernel, out_shape=jax.ShapeDtypeStruct((2 * CENTRES, MEMBE...  132 us

profile of v5, /device:TPU:1, one launch (start us, length us, event | category | flops | bytes accessed | tf_op | source)
XLA Modules:
  0.0 133.5 jit_solution(17807312803346473717)
XLA Ops:
  0.6 131.5 %gauss_newton.1 = f32[64,128]{1,0:T(8,128)} custom-call(bf16[2,8,2,32,512]{4,3,2,1,0:T(8,128)(2,1)} %bitcast.3, s32[1,2]{1,0:T(1,128)} %bitcast.5, s32[4,64]{1,0:T(4,128)} %bitcast.4, s32[1,1024]{1,0:T(1,128)} %centres_hbm.1, f32[32,128]{1,0:T(8,128)} %controls.1, f32[32,128]{1,0:T(8,128)} %observed_hbm.1), custom_call_target="tpu_custom_call" | custom-call | flops 3000000000 | bytes 2000000 | tf_op jit(solution)/shard_map/gauss_newton/pallas_call | solution.py:461
  132.1 1.3 %fusion = (f32[32,128]{1,0:T(8,128)}, f32[32,128]{1,0:T(8,128)}) fusion(f32[64,128]{1,0:T(8,128)} %gauss_newton.1), kind=kLoop, calls=%fused_computation | loop fusion | bytes 65536 | tf_op jit(solution)/shard_map/slice | solution.py:476

commit v6 on v5

--- a/solution.py
+++ b/solution.py
@@ -33,13 +33,13 @@
 def kernel(
     sens_hbm, blocks_hbm, margin_hbm, centres_hbm, controls, observed_hbm, outputs,
     blocks, margin, centres, observed, sens, sens_t, basis, basis_r, basis_t, coeff_rhs, cell_rhs, row_rhs, slope, pulled,
-    list_in, hot, hot_t, same, entry_rhs,
+    list_in, hits, hot, hot_t, same, entry_rhs,
     gath, part, core_in, paired, y_in, full, scat_out, scat_in, ans_out, ans_in,
     own_grad, own_dir, own_image, own_res, own_upd,
-    row_core, row_core_in, row_y, row_y_in, row_s, row_s_in, row_c, row_c_in, pair_out, pair_in,
+    row_core, row_core_in, row_y, row_y_in, row_s, row_s_in, row_c, row_c_in, row_n, row_n_in, row_m, row_m_in, grad_out, grad_in,
     sens_sem, blocks_sem, margin_sem, centres_sem, controls_sem, observed_sem, li_s, li_r, gz_s, gz_r, gx_s, gx_r, hx_s, hx_r, hz_s, hz_r, cc_s, cc_r,
     c_s, c_r, y_s, y_r, fy_s, fy_r, fc_s, fc_r,
-    sc_s, sc_r, an_s, an_r, rc_s, rc_r, ry_s, ry_r, rs_s, rs_r, pr_s, pr_r,
+    sc_s, sc_r, an_s, an_r, rc_s, rc_r, ry_s, ry_r, rs_s, rs_r, nx_s, nx_r, nz_s, nz_r, gr_s, gr_r,
 ):
     stn, cell = lax.axis_index("stn"), lax.axis_index("cell")
     x, z = stn // NZ, stn % NZ
@@ -104,12 +104,13 @@
     for copy in small:
         copy.wait()
     listed = [[margin[o, blocks[0, n]] for o in range(MARGINS)] for n in range(SLOTS)]
-    entry = lax.broadcasted_iota(jnp.int32, (SLOTS * MARGINS, MEMBERS), 0)
-    lists = jnp.zeros((SLOTS * MARGINS, MEMBERS), F32)
+    entry = lax.broadcasted_iota(jnp.int32, (1, MEMBERS), 1)
+    lists = jnp.zeros((1, MEMBERS), F32)
     for n in range(SLOTS):
         for o in range(MARGINS):
             lists = jnp.where(entry == n * MARGINS + o, listed[n][o].astype(F32), lists)
     list_in[stn] = lists
+    grad_out[...] = jnp.zeros_like(grad_out)
 
     lane = lax.broadcasted_iota(jnp.int32, (8, MEMBERS), 1)
     rows_of_centres = [
@@ -170,8 +171,11 @@
 
     def use_lists():
         drain(list_in.at[0:NSTN - 1], li_r)
-        flat_lists = list_in[...].reshape(NSTN * SLOTS * MARGINS, MEMBERS)
-        found = (flat_lists == lax.broadcasted_iota(jnp.int32, flat_lists.shape, 1).astype(F32)).astype(F32)
+        everyones = jnp.concatenate([list_in[i] for i in range(NSTN)], axis=0)
+        number = lax.broadcasted_iota(jnp.int32, (NSTN, MEMBERS), 1).astype(F32)
+        for e in range(SLOTS * MARGINS):
+            hits[:, e, :] = (everyones[:, e:e + 1] == number).astype(F32)
+        found = hits[...].reshape(NSTN * SLOTS * MARGINS, MEMBERS)
         hot[...] = found.astype(BF16)
         found_t = found.T.astype(BF16)
         hot_t[...] = found_t[0:NSTN]
@@ -311,13 +315,21 @@
         ans_in[k, stn] = ans_out[k, stn]
         own = own_change() if step is None else own_grad[...] - step * own_change()
         own_grad[...] = own
-        square = column_sum(own * own)
+        row_n[k] = column_sum(own * own)
+        for peer in x_peers:
+            send(row_n.at[k], row_n_in.at[k, x], nx_s.at[k], nx_r.at[k], peer)
+        row_n_in[k, x] = row_n[k]
         for j in range(NSTN):
-            pair_out[k, j, 0:1] = own[j:j + 1]
-            pair_out[k, j, 1:2] = square
-        for peer in s_peers:
-            send(pair_out.at[k, peer[0]], pair_in.at[k, stn], pr_s.at[k], pr_r.at[k], peer)
-        pair_in[k, stn] = pair_out[k, stn]
+            grad_out[j, k:k + 1] = own[j:j + 1]
+        drain(row_n_in.at[k, 0:NX - 1], nx_r.at[k])
+        row_m[k] = sum(row_n_in[k, i] for i in range(NX))
+        for peer in z_peers:
+            send(row_m.at[k], row_m_in.at[k, z], nz_s.at[k], nz_r.at[k], peer)
+        row_m_in[k, z] = row_m[k]
+        if k == ITERS - 1:
+            for peer in s_peers:
+                send(grad_out.at[peer[0]], grad_in.at[stn], gr_s, gr_r, peer)
+            grad_in[stn] = grad_out[stn]
 
     for n in range(SLOTS):
         for o in range(MARGINS):
@@ -332,7 +344,7 @@
     adjoint(0, False)
     answer(0)
 
-    norm = None
+    norm, ratios, steps = None, [], []
     for k in range(1, ITERS + 1):
         drain(ans_in.at[k - 1, 0:NSTN - 1], an_r.at[k - 1])
         tiles = ans_in[k - 1].reshape(CENTRES // 2, 2, SLOTS * MARGINS, MEMBERS)
@@ -343,8 +355,8 @@
             put_cells(n, slope[n] * fields[n])
 
         def group_norm():
-            drain(pair_in.at[k - 1, 0:NSTN - 1], pr_r.at[k - 1])
-            return sum(pair_in[k - 1, i, 1:2] for i in range(NSTN))
+            drain(row_m_in.at[k - 1, 0:NZ - 1], nz_r.at[k - 1])
+            return sum(row_m_in[k - 1, i] for i in range(NZ))
 
         image, new_norm = sum_cells(k, group_norm)
         ratio = new_norm / norm if k > 1 else None
@@ -358,16 +370,21 @@
             row_c[...] = column_sum(image * image)
             for peer in y_others + y_peers + [core_peer]:
                 send(row_c, row_c_in.at[cell], cc_s, cc_r, peer)
-        direction = jnp.concatenate([pair_in[k - 1, i, 0:1] for i in range(NSTN)], axis=0)
-        if k > 1:
-            direction = direction + ratio * own_dir[...]
-        own_dir[...] = direction
+        ratios.append(ratio)
         if k < ITERS:
             curvature = adjoint(k, True)
             step = norm / curvature
             answer(k, step)
         else:
             row_c_in[cell] = row_c[...]
+            drain(grad_in.at[0:NSTN - 1], gr_r)
+            for i in range(ITERS):
+                direction = jnp.concatenate([grad_in[t, i:i + 1] for t in range(NSTN)], axis=0)
+                if i > 0:
+                    direction = direction + ratios[i] * own_dir[...]
+                own_dir[...] = direction
+                if i < ITERS - 1:
+                    own_upd[...] = steps[i] * direction if i == 0 else own_upd[...] + steps[i] * direction
             drain(row_c_in.at[0:NCELL - 1], cc_r)
             row_s[0] = sum(row_c_in[i] for i in range(NCELL))
             for peer in s_peers:
@@ -376,9 +393,9 @@
             drain(row_s_in.at[0, 0:NSTN - 1], rs_r.at[0])
             step = norm / sum(row_s_in[0, i] for i in range(NSTN))
         own_res[...] = own_res[...] - step * image
-        own_upd[...] = step * direction if k == 1 else own_upd[...] + step * direction
-
-    outputs[0:CENTRES] = gath[x, z] + own_upd[...]
+        steps.append(step)
+
+    outputs[0:CENTRES] = gath[x, z] + (own_upd[...] + steps[-1] * own_dir[...])
     outputs[CENTRES:] = own_res[...]
 
     drain(gath.at[0, 0:NZ - 1, most], gz_s)
@@ -386,6 +403,7 @@
     drain(gath.at[0:NX - 1, 0, rest], hx_s)
     drain(gath.at[:, 0:NZ - 1, rest], hz_s)
     drain(row_c_in.at[0:NCELL - 1], cc_s)
+    drain(grad_in.at[0:NSTN - 1], gr_s)
     drain(list_in.at[0:NSTN - 1], li_s)
     for k in range(ITERS + 1):
         for g in range(2):
@@ -401,7 +419,8 @@
         drain(scat_in.at[k, 0:NSTN - 1], sc_s.at[k])
         drain(ans_in.at[k, 0:NSTN - 1], an_s.at[k])
         drain(row_s_in.at[k, 0:NSTN - 1], rs_s.at[k])
-        drain(pair_in.at[k, 0:NSTN - 1], pr_s.at[k])
+        drain(row_n_in.at[k, 0:NX - 1], nx_s.at[k])
+        drain(row_m_in.at[k, 0:NZ - 1], nz_s.at[k])
 
 
 def local(sensitivity, block_list, margin, centres, controls, observed):
@@ -427,6 +446,7 @@
         pltpu.VMEM((2, BLOCK // 2, 2 * MEMBERS), BF16),
         vmem(SLOTS, BLOCK, MEMBERS),
         vmem(SLOTS, BLOCK, MEMBERS),
+        vmem(NSTN, 1, MEMBERS),
         vmem(NSTN, entries, MEMBERS),
         pltpu.VMEM((NSTN * entries, MEMBERS), BF16),
         pltpu.VMEM((NSTN, NSTN * entries), BF16),
@@ -447,7 +467,9 @@
         vmem(r, 1, MEMBERS), vmem(r, NY, 1, MEMBERS),
         vmem(d, 1, MEMBERS), vmem(d, NSTN, 1, MEMBERS),
         vmem(1, MEMBERS), vmem(NCELL, 1, MEMBERS),
-        vmem(d, NSTN, 2, MEMBERS), vmem(d, NSTN, 2, MEMBERS),
+        vmem(d, 1, MEMBERS), vmem(d, NX, 1, MEMBERS),
+        vmem(d, 1, MEMBERS), vmem(d, NZ, 1, MEMBERS),
+        vmem(NSTN, d + 1, MEMBERS), vmem(NSTN, d + 1, MEMBERS),
     ]
     scratch += [pltpu.SemaphoreType.DMA((2 * SLOTS,))]
     scratch += [pltpu.SemaphoreType.DMA] * 17
@@ -456,7 +478,8 @@
     scratch += [pltpu.SemaphoreType.DMA((2 * d,))] * 4
     scratch += [pltpu.SemaphoreType.DMA((d,))] * 4
     scratch += [pltpu.SemaphoreType.DMA((r,))] * 4
-    scratch += [pltpu.SemaphoreType.DMA((d,))] * 4
+    scratch += [pltpu.SemaphoreType.DMA((d,))] * 6
+    scratch += [pltpu.SemaphoreType.DMA] * 2
     in_vmem = pl.BlockSpec(memory_space=pltpu.VMEM)
     outputs = pl.pallas_call(
         kernel,

time: 134 us -> 133 us (level)
  no operation moved by 1% of the time
where the time goes in v6:
time: 133 us
  Pallas kernels  131 us (98%)
  local copies, waits for them, and re-layouts  1.35 us (1%)
    pallas_call x1, Pallas kernels, local(): pl.pallas_call(kernel, out_shape=jax.ShapeDtypeStruct((2 * CENTRES, MEMBE...  131 us

profile of v6, /device:TPU:1, one launch (start us, length us, event | category | flops | bytes accessed | tf_op | source)
XLA Modules:
  0.0 132.6 jit_solution(5581628142377558293)
XLA Ops:
  0.6 130.6 %gauss_newton.1 = f32[64,128]{1,0:T(8,128)} custom-call(bf16[2,8,2,32,512]{4,3,2,1,0:T(8,128)(2,1)} %bitcast.3, s32[1,2]{1,0:T(1,128)} %bitcast.5, s32[4,64]{1,0:T(4,128)} %bitcast.4, s32[1,1024]{1,0:T(1,128)} %centres_hbm.1, f32[32,128]{1,0:T(8,128)} %controls.1, f32[32,128]{1,0:T(8,128)} %observed_hbm.1), custom_call_target="tpu_custom_call" | custom-call | flops 3000000000 | bytes 2000000 | tf_op jit(solution)/shard_map/gauss_newton/pallas_call | solution.py:484
  131.3 1.3 %fusion = (f32[32,128]{1,0:T(8,128)}, f32[32,128]{1,0:T(8,128)}) fusion(f32[64,128]{1,0:T(8,128)} %gauss_newton.1), kind=kLoop, calls=%fused_computation | loop fusion | bytes 65536 | tf_op jit(solution)/shard_map/slice | solution.py:499

commit v7 on v6

--- a/solution.py
+++ b/solution.py
@@ -19,6 +19,10 @@
     return high, low
 
 
+def wide(value):
+    return jnp.concatenate(split(value), axis=1)
+
+
 def column_sum(value):
     return jnp.sum(value.reshape(-1, MEMBERS), axis=0, keepdims=True)
 
@@ -32,7 +36,7 @@
 
 def kernel(
     sens_hbm, blocks_hbm, margin_hbm, centres_hbm, controls, observed_hbm, outputs,
-    blocks, margin, centres, observed, sens, sens_t, basis, basis_r, basis_t, coeff_rhs, cell_rhs, row_rhs, slope, pulled,
+    blocks, margin, centres, observed, sens, sens_t, basis, basis_r, basis_t, coeff_rhs, cell_rhs, slope, pulled,
     list_in, hits, hot, hot_t, same, entry_rhs,
     gath, part, core_in, paired, y_in, full, scat_out, scat_in, ans_out, ans_in,
     own_grad, own_dir, own_image, own_res, own_upd,
@@ -195,10 +199,11 @@
         both = jnp.dot(left, rhs, preferred_element_type=F32)
         return both[:, 0:MEMBERS] + both[:, MEMBERS:]
 
-    def station_rows(half):
-        both = jnp.dot(sens[half, 0].reshape(BLOCK // 2, BLOCK), cell_rhs[0], preferred_element_type=F32)
-        both += jnp.dot(sens[half, 1].reshape(BLOCK // 2, BLOCK), cell_rhs[1], preferred_element_type=F32)
-        return (both[:, 0:MEMBERS] + both[:, MEMBERS:]).reshape(NY, CENTRES, MEMBERS)
+    def station_rows(half, at=slice(0, NY)):
+        count = (at.stop - at.start) * CENTRES
+        both = jnp.dot(sens[half, 0, at].reshape(count, BLOCK), cell_rhs[0], preferred_element_type=F32)
+        both += jnp.dot(sens[half, 1, at].reshape(count, BLOCK), cell_rhs[1], preferred_element_type=F32)
+        return (both[:, 0:MEMBERS] + both[:, MEMBERS:]).reshape(-1, CENTRES, MEMBERS)
 
     def put_cells(n, value):
         high, low = split(value)
@@ -220,8 +225,8 @@
     place = {d: p for p, d in enumerate(far_y + [0])}
 
     def sum_cells(k, group_norm=None, meanwhile=None):
-        part[k] = station_rows(0)
         for g, blocks_of in enumerate(groups):
+            part[k, blocks_of] = station_rows(0, blocks_of)
             send(part.at[k, blocks_of], core_in.at[k, blocks_of], c_s.at[2 * k + g], c_r.at[2 * k + g], core_peer)
         own_rows = station_rows(1)
         if group_norm is not None:
@@ -256,13 +261,8 @@
                 send(row_s.at[k], row_s_in.at[k, stn], rs_s.at[k], rs_r.at[k], peer)
             row_s_in[k, stn] = row_s[k]
 
-    def pull(half):
-        return both_ways(sens_t[half], row_rhs[half]).reshape(SLOTS, BLOCK, MEMBERS)
-
-    def put_rows(half, value):
-        high, low = split(value)
-        row_rhs[half, :, 0:MEMBERS] = high
-        row_rhs[half, :, MEMBERS:] = low
+    def pull(half, rows):
+        return both_ways(sens_t[half], wide(rows)).reshape(SLOTS, BLOCK, MEMBERS)
 
     def adjoint(k, with_curvature):
         for g, arrived in ((1, slice(3, NY - 1)), (0, slice(0, 3))):
@@ -271,23 +271,20 @@
                 full.at[k, 1, groups[g]], full.at[k, 0, groups[g]],
                 fc_s.at[2 * k + g], fc_r.at[2 * k + g], core_peer,
             )
-        put_rows(1, full[k, 1].reshape(BLOCK // 2, MEMBERS))
-        pulled[...] = pull(1)
+        pulled[...] = pull(1, full[k, 1].reshape(BLOCK // 2, MEMBERS))
         if with_curvature:
             drain(row_s_in.at[k, 0:NSTN - 1], rs_r.at[k])
             row_core[ITERS + k] = sum(row_s_in[k, i] for i in range(NSTN))
             send(row_core.at[ITERS + k], row_core_in.at[ITERS + k], rc_s.at[ITERS + k], rc_r.at[ITERS + k], core_peer)
         for g in (1, 0):
             drain(full.at[k, 0, groups[g]], fc_r.at[2 * k + g])
-        put_rows(0, full[k, 0].reshape(BLOCK // 2, MEMBERS))
-        rest_of = pull(0)
-        for n in range(SLOTS):
-            put_cells(n, slope[n] * (pulled[n] + rest_of[n]))
+        rest_of = pull(0, full[k, 0].reshape(BLOCK // 2, MEMBERS))
+        weighted = [wide(slope[n] * (pulled[n] + rest_of[n])) for n in range(SLOTS)]
         if with_curvature:
             share_row(ITERS + k)
         parts = []
         for n in range(SLOTS):
-            two = both_ways(basis_t[n], cell_rhs[n])
+            two = both_ways(basis_t[n], weighted[n])
             parts.append((two[0:MEMBERS] + two[MEMBERS:]).reshape(CENTRES // 2, 2 * MARGINS, MEMBERS))
         even, odd = interleave(parts[0], parts[1])
         scat_out[k, :, 0] = even
@@ -443,7 +440,6 @@
         pltpu.VMEM((SLOTS, 2 * MEMBERS, BLOCK), BF16),
         pltpu.VMEM((SLOTS, 2 * MEMBERS, 2 * MEMBERS), BF16),
         pltpu.VMEM((SLOTS, BLOCK, 2 * MEMBERS), BF16),
-        pltpu.VMEM((2, BLOCK // 2, 2 * MEMBERS), BF16),
         vmem(SLOTS, BLOCK, MEMBERS),
         vmem(SLOTS, BLOCK, MEMBERS),
         vmem(NSTN, 1, MEMBERS),

time: 133 us -> 133 us (level)
  no operation moved by 1% of the time
where the time goes in v7:
time: 133 us; the launch traced here: 132 us
  Pallas kernels  130 us (98%)
  local copies, waits for them, and re-layouts  1.35 us (1%)
    pallas_call x1, Pallas kernels, local(): pl.pallas_call(kernel, out_shape=jax.ShapeDtypeStruct((2 * CENTRES, MEMBE...  130 us

profile of v7, /device:TPU:1, one launch (start us, length us, event | category | flops | bytes accessed | tf_op | source)
XLA Modules:
  0.0 132.5 jit_solution(14380246608680366059)
XLA Ops:
  0.6 130.5 %gauss_newton.1 = f32[64,128]{1,0:T(8,128)} custom-call(bf16[2,8,2,32,512]{4,3,2,1,0:T(8,128)(2,1)} %bitcast.3, s32[1,2]{1,0:T(1,128)} %bitcast.5, s32[4,64]{1,0:T(4,128)} %bitcast.4, s32[1,1024]{1,0:T(1,128)} %centres_hbm.1, f32[32,128]{1,0:T(8,128)} %controls.1, f32[32,128]{1,0:T(8,128)} %observed_hbm.1), custom_call_target="tpu_custom_call" | custom-call | flops 3000000000 | bytes 2000000 | tf_op jit(solution)/shard_map/gauss_newton/pallas_call | solution.py:480
  131.1 1.3 %fusion = (f32[32,128]{1,0:T(8,128)}, f32[32,128]{1,0:T(8,128)}) fusion(f32[64,128]{1,0:T(8,128)} %gauss_newton.1), kind=kLoop, calls=%fused_computation | loop fusion | bytes 65536 | tf_op jit(solution)/shard_map/slice | solution.py:495

commit v8 on v7

--- a/solution.py
+++ b/solution.py
@@ -229,14 +229,14 @@
             part[k, blocks_of] = station_rows(0, blocks_of)
             send(part.at[k, blocks_of], core_in.at[k, blocks_of], c_s.at[2 * k + g], c_r.at[2 * k + g], core_peer)
         own_rows = station_rows(1)
-        if group_norm is not None:
-            row_core[k] = group_norm()
-            send(row_core.at[k], row_core_in.at[k], rc_s.at[k], rc_r.at[k], core_peer)
         for g, blocks_of in enumerate(groups):
             drain(core_in.at[k, blocks_of], c_r.at[2 * k + g])
             paired[k, blocks_of] = own_rows[blocks_of] + core_in[k, blocks_of]
             for p, peer in list(enumerate(y_peers))[blocks_of]:
                 send(paired.at[k, p], y_in.at[k, y], y_s.at[k], y_r.at[k], peer)
+            if g == 0 and group_norm is not None:
+                row_core[k] = group_norm()
+                send(row_core.at[k], row_core_in.at[k], rc_s.at[k], rc_r.at[k], core_peer)
         y_in[k, y] = paired[k, NY - 1]
         if meanwhile is not None:
             meanwhile()

time: 133 us -> 133 us (level)
  no operation moved by 1% of the time
where the time goes in v8:
time: 133 us
  Pallas kernels  131 us (98%)
  local copies, waits for them, and re-layouts  1.35 us (1%)
    pallas_call x1, Pallas kernels, local(): pl.pallas_call(kernel, out_shape=jax.ShapeDtypeStruct((2 * CENTRES, MEMBE...  131 us

profile of v8, /device:TPU:1, one launch (start us, length us, event | category | flops | bytes accessed | tf_op | source)
XLA Modules:
  0.0 132.5 jit_solution(7481810528699058533)
XLA Ops:
  0.6 130.5 %gauss_newton.1 = f32[64,128]{1,0:T(8,128)} custom-call(bf16[2,8,2,32,512]{4,3,2,1,0:T(8,128)(2,1)} %bitcast.3, s32[1,2]{1,0:T(1,128)} %bitcast.5, s32[4,64]{1,0:T(4,128)} %bitcast.4, s32[1,1024]{1,0:T(1,128)} %centres_hbm.1, f32[32,128]{1,0:T(8,128)} %controls.1, f32[32,128]{1,0:T(8,128)} %observed_hbm.1), custom_call_target="tpu_custom_call" | custom-call | flops 3000000000 | bytes 2000000 | tf_op jit(solution)/shard_map/gauss_newton/pallas_call | solution.py:480
  131.2 1.3 %fusion = (f32[32,128]{1,0:T(8,128)}, f32[32,128]{1,0:T(8,128)}) fusion(f32[64,128]{1,0:T(8,128)} %gauss_newton.1), kind=kLoop, calls=%fused_computation | loop fusion | bytes 65536 | tf_op jit(solution)/shard_map/slice | solution.py:495
